TPU v7x, 256 devices: a whole 4x4x8 slice. The times are simulated.
256 devices in a mesh: slope: 32 (over z_lo, x, core), cross: 8 (over y, z_hi).
Axes of the slice: x: 4, y: 4, z: 8 (z_hi: 2, z_lo: 4; z = z_hi * 4 + z_lo), core: 2. Of those that a mesh axis runs over, the one named last changes fastest.
Arguments:
- offsets: float32 [3, 32, 8, 4096], P(None, 'slope', 'cross'), may hold values from 0.5 to 4.5
- velocity: float32 [3, 32, 8, 4096], P(None, 'slope', 'cross'), may hold values from -4 to 4
- affine: float32 [9, 32, 8, 4096], P(None, 'slope', 'cross'), may hold values from -4 to 4
- strain: float32 [9, 32, 8, 4096], P(None, 'slope', 'cross'), may hold values from -1.5 to 1.5
- particle_mass: float32 [32, 8, 4096], P('slope', 'cross'), may hold values from 0.5 to 2
- plastic_ratio: float32 [32, 8, 4096], P('slope', 'cross'), may hold values from 0.85 to 1.15
- block_counts: int32 [32, 8, 8], P('slope', 'cross'), may hold values from 1 to 512, as said below
Outputs:
- offsets_out: float32 [3, 32, 8, 4096], P(None, 'slope', 'cross')
- velocity_out: float32 [3, 32, 8, 4096], P(None, 'slope', 'cross')
- affine_out: float32 [9, 32, 8, 4096], P(None, 'slope', 'cross')
- deformation: float32 [9, 32, 8, 4096], P(None, 'slope', 'cross')
Inputs may be any that keep to these rules, and one draw needn't show every extreme that they name: `block_counts`: the lowest block (k = 0) of every column holds 512 live particles.
All inputs are finite; a program needn't handle non-finite values.
Results may differ from a plain program's by a relative error of at most 0.0003.
Values sent between devices are 32-bit elements; how exact they have to be, the bound alone decides.
A program may use at most 64 MiB of HBM per device.

v0:
```python
import functools

import jax
import jax.numpy as jnp
from jax import lax
from jax.experimental import pallas as pl
from jax.experimental.pallas import tpu as pltpu
from jax.sharding import PartitionSpec as P

STEPS = 5
BLOCKS = 8
ROWS = 32
CHUNKS = 4
TILES = 4
VMEM_BYTES = 60 * 1024 * 1024
MESH = pl.DeviceIdType.MESH

time_step = 0.02
shear_modulus = 4.0
lame_lambda = 4.0
hardening = 10.0
mass_floor = 0.25
gravity_slope = 1.5
gravity_vertical = -2.5
CENTRE = 2.5

DIRECTIONS = [(0, -1), (0, 1), (-1, -1), (-1, 1), (1, -1), (1, 1), (-1, 0), (1, 0)]


def iota(shape, dim):
    return lax.broadcasted_iota(jnp.int32, shape, dim)


def axis_weights(position):
    base = jnp.floor(position + 0.5)
    dist = position - base
    lower = 0.5 * (0.5 - dist) * (0.5 - dist)
    middle = 0.75 - dist * dist
    upper = 0.5 * (0.5 + dist) * (0.5 + dist)
    at = {e: base == float(e) for e in range(-1, 7)}
    return [
        jnp.where(at[e], middle, jnp.where(at[e + 1], lower, jnp.where(at[e - 1], upper, 0.0)))
        for e in range(6)
    ]


def split(values):
    high = values.astype(jnp.bfloat16)
    low = (values - high.astype(jnp.float32)).astype(jnp.bfloat16)
    return high, low


def kernel(
    nx, ny,
    counts, off_hbm, vel_hbm, aff_hbm, strain_hbm, mass_hbm, plastic_hbm,
    off, vel, aff, frame,
    strain_in, mass_in, plastic_in, live_ref, mw_ref, hard_ref, wx, wy, wz, feats, bs, us, gathered,
    send_x, send_low, send_high, recv_x, recv_low, recv_high, diag_low, diag_high,
    load_sem, send_sem, recv_sem,
):
    ix = lax.axis_index("slope")
    iy = lax.axis_index("cross")

    def present(dx, dy):
        ok = None
        for d, i, n in ((dx, ix, nx), (dy, iy, ny)):
            if d == 0:
                continue
            here = (i + d >= 0) & (i + d < n)
            ok = here if ok is None else ok & here
        return ok

    loads = [
        pltpu.make_async_copy(source, target, load_sem.at[i])
        for i, (source, target) in enumerate((
            (mass_hbm, mass_in), (plastic_hbm, plastic_in), (off_hbm, off), (vel_hbm, vel),
            (aff_hbm, aff), (strain_hbm, strain_in),
        ))
    ]
    for load in loads:
        load.start()

    for ref in (recv_x, recv_low, recv_high, diag_low, diag_high, wx, wz, us, bs):
        ref[...] = jnp.zeros(ref.shape, ref.dtype)

    barrier = pltpu.get_barrier_semaphore()
    around = jnp.int32(0)
    for dx, dy in DIRECTIONS:
        ok = present(dx, dy)

        @pl.when(ok)
        def _():
            pl.semaphore_signal(barrier, inc=1, device_id=(ix + dx, iy + dy), device_id_type=MESH)

        around = around + jnp.where(ok, 1, 0).astype(jnp.int32)

    row = iota((ROWS, 128), 0)
    slot = (row % CHUNKS) * 128 + iota((ROWS, 128), 1)
    limit = jnp.zeros((ROWS, 128), jnp.int32)
    for k in range(BLOCKS):
        limit = jnp.where(row // CHUNKS == k, counts[k], limit)
    live = jnp.where(slot < limit, 1.0, 0.0).astype(jnp.float32)
    live_ref[...] = live
    for load in loads:
        load.wait()
    mw_ref[...] = mass_in[...] * live
    hard_ref[...] = 4.0 * time_step * live * jnp.exp(hardening * (1.0 - plastic_in[...]))
    for i in range(9):
        frame[i] = strain_in[i] + (1.0 if i % 4 == 0 else 0.0)

    pl.semaphore_wait(barrier, around)

    lane = iota((8, 128), 1)
    sub = iota((8, 128), 0)
    half = lane < 64
    r3 = lane % 8
    e2 = (lane % 64) // 8
    e3 = jnp.where(half, r3, (r3 + 4) % 8)
    ex = sub.astype(jnp.float32) - CENTRE
    ey = e2.astype(jnp.float32) - CENTRE
    ez = e3.astype(jnp.float32) - CENTRE
    own = half | (r3 >= 4)
    group = (lane % 64) // 16

    def copy_to(step, d):
        dx, dy = DIRECTIONS[d]
        back = DIRECTIONS.index((-dx, -dy))
        if dy == 0:
            source, target = send_x, recv_x
        elif dx == 0:
            source, target = (send_low, recv_high) if dy < 0 else (send_high, recv_low)
        else:
            source, target = (send_low, diag_high) if dy < 0 else (send_high, diag_low)
        source, target = source.at[step], target.at[step]
        if dx != 0:
            source = source.at[:, pl.ds(0 if dx < 0 else 4, 2), :]
            target = target.at[:, pl.ds(4 if dx < 0 else 0, 2), :]
        else:
            source = source.at[:, pl.ds(0, 6), :]
            target = target.at[:, pl.ds(0, 6), :]
        return pltpu.make_async_remote_copy(
            src_ref=source, dst_ref=target,
            send_sem=send_sem.at[step, d], recv_sem=recv_sem.at[step, back],
            device_id=(ix + dx, iy + dy), device_id_type=MESH,
        )

    def spread(ref, at):
        return jnp.broadcast_to(ref[pl.ds(at, 1), :], (8, 128))

    def one_step(step, carry):
        o = [off[i] for i in range(3)]
        f = [frame[i] for i in range(9)]
        det = (
            f[0] * (f[4] * f[8] - f[5] * f[7])
            - f[1] * (f[3] * f[8] - f[5] * f[6])
            + f[2] * (f[3] * f[7] - f[4] * f[6])
        )
        bulk = lame_lambda * (det - 1.0) * det
        mw = mw_ref[...]
        hard = hard_ref[...]
        centred = [v - CENTRE for v in o]
        terms = [[None] * 3 for _ in range(3)]
        for a in range(3):
            for b in range(a, 3):
                stretch = f[3 * a] * f[3 * b] + f[3 * a + 1] * f[3 * b + 1] + f[3 * a + 2] * f[3 * b + 2]
                if a == b:
                    tau = hard * (shear_modulus * (stretch - 1.0) + bulk)
                else:
                    tau = hard * (shear_modulus * stretch)
                terms[a][b] = mw * aff[3 * a + b] - tau
                if a != b:
                    terms[b][a] = mw * aff[3 * b + a] - tau
        feats[pl.ds(0, ROWS), :] = mw
        for a in range(3):
            moved = terms[a][0] * centred[0] + terms[a][1] * centred[1] + terms[a][2] * centred[2]
            feats[pl.ds((1 + a) * ROWS, ROWS), :] = mw * vel[a] - moved
            for b in range(3):
                feats[pl.ds((4 + 3 * b + a) * ROWS, ROWS), :] = terms[a][b]
        for e, w in enumerate(axis_weights(o[0])):
            wx[pl.ds(e * ROWS, ROWS), :] = w
        for e, w in enumerate(axis_weights(o[1])):
            wy[pl.ds(e * ROWS, ROWS), :] = w
        for e, w in enumerate(axis_weights(o[2])):
            wz[pl.ds((4 + e) * ROWS, ROWS), :] = w
            if e >= 4:
                wz[pl.ds((e - 4) * ROWS, ROWS), :] = w

        summed = []
        for k in range(BLOCKS):
            sides, planes = [], []
            for c in range(CHUNKS):
                r = CHUNKS * k + c
                wxs = wx[pl.ds(r, 8, stride=ROWS), :]
                wzs = wz[pl.ds(r + (4 * ROWS if k % 2 == 0 else 0), 8, stride=ROWS), :]
                planes.append(
                    jnp.concatenate([spread(wy, e * ROWS + r) * wzs for e in range(6)], axis=0)
                )
                part = [spread(feats, i * ROWS + r) for i in range(13)]
                side = [part[0] * wxs]
                side += [(part[1 + a] + part[4 + a] * ex) * wxs for a in range(3)]
                side += [part[7 + i] * wxs for i in range(6)]
                sides.append(jnp.concatenate(side, axis=0))
            plane_high, plane_low = split(jnp.concatenate(planes, axis=1))
            bs[k, 0:48, :] = plane_high
            bs[k, 64:112, :] = plane_low
            side_high, side_low = split(jnp.concatenate(sides, axis=1))
            dots = lax.dot_general(
                jnp.concatenate([side_high, side_low], axis=0), bs[k],
                (((1,), (1,)), ((), ())), preferred_element_type=jnp.float32,
            )
            total = dots[:80] + dots[80:]
            summed.append(total + pltpu.roll(total, 64, 1))

        fields = []
        for j in range(TILES):
            pair = [
                jnp.where(half, summed[2 * j][8 * i : 8 * i + 8], summed[2 * j + 1][8 * i : 8 * i + 8])
                for i in range(10)
            ]
            fields.append(
                [pair[0]] + [pair[1 + a] + ey * pair[4 + a] + ez * pair[7 + a] for a in range(3)]
            )
        zero = jnp.zeros((8, 128), jnp.float32)
        shifted = [
            [jnp.where(own, fields[j][i], fields[j - 1][i] if j else zero) for i in range(4)]
            for j in range(TILES)
        ]
        mine = {}
        for p in range(2):
            for i in range(4):
                first, second = shifted[2 * p][i], shifted[2 * p + 1][i]
                mine[i, p] = jnp.where(half, first, second) + pltpu.roll(
                    jnp.where(half, second, first), 64, 1
                )
                send_x[step, 2 * i + p] = mine[i, p]
            low, high = zero, zero
            for i in range(4):
                to_low = mine[i, p] if i == 0 else pltpu.roll(mine[i, p], 16 * i, 1)
                shift = (16 * i - 32) % 128
                to_high = mine[i, p] if shift == 0 else pltpu.roll(mine[i, p], shift, 1)
                low = jnp.where(group == i, to_low, low)
                high = jnp.where(group == i, to_high, high)
            send_low[step, p] = low
            send_high[step, p] = high

        for d, (dx, dy) in enumerate(DIRECTIONS):

            @pl.when(present(dx, dy))
            def _():
                copy_to(step, d).start()

        for d, (dx, dy) in enumerate(DIRECTIONS):

            @pl.when(present(dx, dy))
            def _():
                copy_to(step, DIRECTIONS.index((-dx, -dy))).wait_recv()

        velocity = {}
        place_x = 4 * ix + sub
        place_y = 4 * iy + e2
        outside = (place_x >= 4 * nx) | (place_y >= 4 * ny)
        for p in range(2):
            below = recv_low[step, p] + diag_low[step, p]
            above = recv_high[step, p] + diag_high[step, p]
            total = []
            for i in range(4):
                from_low = below if i == 0 else pltpu.roll(below, 128 - 16 * i, 1)
                shift = (32 - 16 * i) % 128
                from_high = above if shift == 0 else pltpu.roll(above, shift, 1)
                extra = jnp.where(group == 0, from_low, jnp.where(group == 2, from_high, 0.0))
                total.append(mine[i, p] + recv_x[step, 2 * i + p] + extra)
            scale = 1.0 / jnp.maximum(total[0], mass_floor)
            speed_x = total[1] * scale + time_step * gravity_slope
            speed_y = total[2] * scale
            speed_z = total[3] * scale + time_step * gravity_vertical
            place_z = 16 * p + jnp.where(half, 0, 8) + r3
            speed_x = jnp.where(place_x < 2, jnp.maximum(speed_x, 0.0), speed_x)
            speed_x = jnp.where(place_x >= 4 * nx - 2, jnp.minimum(speed_x, 0.0), speed_x)
            speed_y = jnp.where(place_y < 2, jnp.maximum(speed_y, 0.0), speed_y)
            speed_y = jnp.where(place_y >= 4 * ny - 2, jnp.minimum(speed_y, 0.0), speed_y)
            speed_z = jnp.where(place_z >= 8 * TILES - 2, jnp.minimum(speed_z, 0.0), speed_z)
            still = outside | (place_z < 2)
            for a, speed in enumerate((speed_x, speed_y, speed_z)):
                velocity[a, p] = jnp.where(still, 0.0, speed)

        turned = {key: pltpu.roll(value, 64, 1) for key, value in velocity.items()}
        for a in range(3):
            turned[a, 2] = zero
        for j in range(TILES):
            p = j // 2
            for a in range(3):
                if j % 2 == 0:
                    window = jnp.where(half | (r3 < 4), velocity[a, p], turned[a, p])
                else:
                    window = jnp.where(
                        half, turned[a, p], jnp.where(r3 >= 4, velocity[a, p], turned[a, p + 1])
                    )
                for b, factor in enumerate((None, ex, ey, ez)):
                    q = 3 * b + a
                    value = window if factor is None else window * factor
                    if q < 8:
                        us[j, pl.ds(q, 6, stride=8), :] = value[:6]
                    else:
                        us[j, pl.ds(48 + q - 8, 6, stride=4), :] = value[:6]

        half80 = iota((80, 128), 1) < 64
        for j in range(TILES):
            both = us[j]
            swapped = pltpu.roll(both, 64, 1)
            for k in (2 * j, 2 * j + 1):
                nodes = jnp.where(half80, both, swapped) if k % 2 == 0 else jnp.where(half80, swapped, both)
                left = jnp.concatenate(split(nodes), axis=1)
                planes = bs[k]
                taken = lax.dot_general(
                    left, jnp.concatenate([planes, planes], axis=0),
                    (((1,), (0,)), ((), ())), preferred_element_type=jnp.float32,
                )
                for c in range(CHUNKS):
                    r = CHUNKS * k + c
                    part = taken[:, 128 * c : 128 * c + 128]
                    weights = [spread(wx, e * ROWS + r) for e in range(6)]
                    first = weights[0] * part[0:8]
                    for e in range(1, 6):
                        first = first + weights[e] * part[8 * e : 8 * e + 8]
                    second = jnp.where(sub < 4, weights[0], weights[1]) * part[48:56]
                    for e in (2, 4):
                        at = 48 + 4 * e
                        second = second + jnp.where(sub < 4, weights[e], weights[e + 1]) * part[at : at + 8]
                    gathered[pl.ds(16 * r, 8), :] = first
                    gathered[pl.ds(16 * r + 8, 8), :] = second

        def quantity(q):
            value = gathered[pl.ds(q, ROWS, stride=16), :]
            if q >= 8:
                value = value + gathered[pl.ds(q + 4, ROWS, stride=16), :]
            return value

        speed = [quantity(a) for a in range(3)]
        change = [None] * 9
        for a in range(3):
            for b in range(3):
                change[3 * a + b] = 4.0 * (quantity(3 + 3 * b + a) - speed[a] * centred[b])
        for a in range(3):
            off[a] = o[a] + time_step * speed[a]
            vel[a] = speed[a]
            for b in range(3):
                aff[3 * a + b] = change[3 * a + b]
                frame[3 * a + b] = f[3 * a + b] + time_step * (
                    change[3 * a] * f[b] + change[3 * a + 1] * f[3 + b] + change[3 * a + 2] * f[6 + b]
                )
        return carry

    lax.fori_loop(0, STEPS, one_step, 0)

    def finish(step, carry):
        for d, (dx, dy) in enumerate(DIRECTIONS):

            @pl.when(present(dx, dy))
            def _():
                copy_to(step, d).wait_send()

        return carry

    lax.fori_loop(0, STEPS, finish, 0)
    live = live_ref[...]
    for ref, count in ((off, 3), (vel, 3), (aff, 9), (frame, 9)):
        for i in range(count):
            ref[i] = ref[i] * live


def write_out(off, vel, aff, frame, off_out, vel_out, aff_out, frame_out, sem):
    copies = [
        pltpu.make_async_copy(source, target, sem.at[i])
        for i, (source, target) in enumerate(
            ((aff, aff_out), (frame, frame_out), (off, off_out), (vel, vel_out))
        )
    ]
    for copy in copies:
        copy.start()
    for copy in copies:
        copy.wait()


def per_device(offsets, velocity, affine, strain, particle_mass, plastic_ratio, block_counts):
    nx, ny = lax.axis_size("slope"), lax.axis_size("cross")
    f32 = jnp.float32
    vmem = pl.BlockSpec(memory_space=pltpu.VMEM)
    smem = pl.BlockSpec(memory_space=pltpu.SMEM)
    hbm = pl.BlockSpec(memory_space=pltpu.HBM)
    outs = pl.pallas_call(
        functools.partial(kernel, nx, ny),
        out_shape=[jax.ShapeDtypeStruct((n, ROWS, 128), f32) for n in (3, 3, 9, 9)],
        in_specs=[smem] + [hbm] * 6,
        out_specs=[vmem] * 4,
        scratch_shapes=[
            pltpu.VMEM((9, ROWS, 128), f32),
            pltpu.VMEM((ROWS, 128), f32),
            pltpu.VMEM((ROWS, 128), f32),
            pltpu.VMEM((ROWS, 128), f32),
            pltpu.VMEM((ROWS, 128), f32),
            pltpu.VMEM((ROWS, 128), f32),
            pltpu.VMEM((8 * ROWS, 128), f32),
            pltpu.VMEM((6 * ROWS, 128), f32),
            pltpu.VMEM((12 * ROWS, 128), f32),
            pltpu.VMEM((13 * ROWS, 128), f32),
            pltpu.VMEM((BLOCKS, 128, 512), jnp.bfloat16),
            pltpu.VMEM((TILES, 80, 128), f32),
            pltpu.VMEM((16 * ROWS, 128), f32),
            pltpu.VMEM((STEPS, 8, 8, 128), f32),
            pltpu.VMEM((STEPS, 2, 8, 128), f32),
            pltpu.VMEM((STEPS, 2, 8, 128), f32),
            pltpu.VMEM((STEPS, 8, 8, 128), f32),
            pltpu.VMEM((STEPS, 2, 8, 128), f32),
            pltpu.VMEM((STEPS, 2, 8, 128), f32),
            pltpu.VMEM((STEPS, 2, 8, 128), f32),
            pltpu.VMEM((STEPS, 2, 8, 128), f32),
            pltpu.SemaphoreType.DMA((6,)),
            pltpu.SemaphoreType.DMA((STEPS, 8)),
            pltpu.SemaphoreType.DMA((STEPS, 8)),
        ],
        compiler_params=pltpu.CompilerParams(
            collective_id=0, has_side_effects=True, vmem_limit_bytes=VMEM_BYTES
        ),
    )(
        block_counts.reshape(BLOCKS),
        offsets.reshape(3, ROWS, 128),
        velocity.reshape(3, ROWS, 128),
        affine.reshape(9, ROWS, 128),
        strain.reshape(9, ROWS, 128),
        particle_mass.reshape(ROWS, 128),
        plastic_ratio.reshape(ROWS, 128),
    )
    outs = pl.pallas_call(
        write_out,
        out_shape=[jax.ShapeDtypeStruct(out.shape, f32) for out in outs],
        in_specs=[hbm] * 4,
        out_specs=[hbm] * 4,
        scratch_shapes=[pltpu.SemaphoreType.DMA((4,))],
        compiler_params=pltpu.CompilerParams(vmem_limit_bytes=VMEM_BYTES),
    )(*outs)
    return tuple(out.reshape(out.shape[0], 1, 1, ROWS * 128) for out in outs)


def solution(mesh):
    wide = P(None, "slope", "cross", None)
    flat = P("slope", "cross", None)
    return jax.shard_map(
        per_device,
        mesh=mesh,
        in_specs=(wide, wide, wide, wide, flat, flat, flat),
        out_specs=(wide, wide, wide, wide),
        check_vma=False,
    )
```

profile of v0, /device:TPU:1, one launch (start us, length us, event | category | flops | bytes accessed | tf_op | source)
XLA Modules:
  0.0 58.3 jit_solution(7799893992793926568)
XLA Ops:
  0.6 44.6 %shard_map.102 = (f32[3,32,128]{2,1,0:T(8,128)}, f32[3,32,128]{2,1,0:T(8,128)}, f32[9,32,128]{2,1,0:T(8,128)}, f32[9,32,128]{2,1,0:T(8,128)}) custom-call(s32[8]{0:T(128)} %bitcast.17, f32[3,32,128]{2,1,0:T(8,128)} %bitcast.13, f32[3,32,128]{2,1,0:T(8,128)} %bitcast.14, f32[9,32,128]{2,1,0:T(8,128)} %bitcast.11, f32[9,32,128]{2,1,0:T(8,128)} %bitcast.12, ...), custom_call_target="tpu_custom_call" | custom-call | tf_op jit(solution)/shard_map/pallas_call | solution.py:390
  45.2 13.1 %shard_map.103 = (f32[3,32,128]{2,1,0:T(8,128)}, f32[3,32,128]{2,1,0:T(8,128)}, f32[9,32,128]{2,1,0:T(8,128)}, f32[9,32,128]{2,1,0:T(8,128)}) custom-call(f32[3,32,128]{2,1,0:T(8,128)} %get-tuple-element.12.off, f32[3,32,128]{2,1,0:T(8,128)} %get-tuple-element.13.vel, f32[9,32,128]{2,1,0:T(8,128)} %get-tuple-element.14.aff, ...), custom_call_target="tpu_custom_call" | custom-call | tf_op jit(solution)/shard_map/pallas_call | solution.py:433
where the time goes:
time: 58.4 us; the launch traced here: 58.3 us
  Pallas kernels  57.6 us (99%)
  between operations  0.64 us (1%)
    pallas_call x1, Pallas kernels, per_device(): pl.pallas_call(functools.partial(kernel, nx, ny), out_shape=[jax.ShapeDty...  44.6 us
    pallas_call x1, Pallas kernels, per_device(): pl.pallas_call(write_out, out_shape=[jax.ShapeDtypeStruct(out.shape, f32)...  13.1 us

commit v1 on v0

--- a/solution.py
+++ b/solution.py
@@ -12,7 +12,7 @@
 ROWS = 32
 CHUNKS = 4
 TILES = 4
-VMEM_BYTES = 60 * 1024 * 1024
+VMEM_BYTES = 40 * 1024 * 1024
 MESH = pl.DeviceIdType.MESH
 
 time_step = 0.02
@@ -52,9 +52,9 @@
 
 def kernel(
     nx, ny,
-    counts, off_hbm, vel_hbm, aff_hbm, strain_hbm, mass_hbm, plastic_hbm,
+    counts_hbm, off_hbm, vel_hbm, aff_hbm, strain_hbm, mass_hbm, plastic_hbm,
     off, vel, aff, frame,
-    strain_in, mass_in, plastic_in, live_ref, mw_ref, hard_ref, wx, wy, wz, feats, bs, us, gathered,
+    counts, strain_in, mass_in, plastic_in, live_ref, mw_ref, hard_ref, wx, wy, wz, feats, bs, us, gathered,
     send_x, send_low, send_high, recv_x, recv_low, recv_high, diag_low, diag_high,
     load_sem, send_sem, recv_sem,
 ):
@@ -73,14 +73,14 @@
     loads = [
         pltpu.make_async_copy(source, target, load_sem.at[i])
         for i, (source, target) in enumerate((
-            (mass_hbm, mass_in), (plastic_hbm, plastic_in), (off_hbm, off), (vel_hbm, vel),
+            (counts_hbm, counts), (mass_hbm, mass_in), (plastic_hbm, plastic_in), (off_hbm, off), (vel_hbm, vel),
             (aff_hbm, aff), (strain_hbm, strain_in),
         ))
     ]
     for load in loads:
         load.start()
 
-    for ref in (recv_x, recv_low, recv_high, diag_low, diag_high, wx, wz, us, bs):
+    for ref in (recv_x, recv_low, recv_high, diag_low, diag_high):
         ref[...] = jnp.zeros(ref.shape, ref.dtype)
 
     barrier = pltpu.get_barrier_semaphore()
@@ -94,6 +94,10 @@
 
         around = around + jnp.where(ok, 1, 0).astype(jnp.int32)
 
+    for ref in (wx, wz, us, bs):
+        ref[...] = jnp.zeros(ref.shape, ref.dtype)
+    for load in loads:
+        load.wait()
     row = iota((ROWS, 128), 0)
     slot = (row % CHUNKS) * 128 + iota((ROWS, 128), 1)
     limit = jnp.zeros((ROWS, 128), jnp.int32)
@@ -101,14 +105,10 @@
         limit = jnp.where(row // CHUNKS == k, counts[k], limit)
     live = jnp.where(slot < limit, 1.0, 0.0).astype(jnp.float32)
     live_ref[...] = live
-    for load in loads:
-        load.wait()
     mw_ref[...] = mass_in[...] * live
     hard_ref[...] = 4.0 * time_step * live * jnp.exp(hardening * (1.0 - plastic_in[...]))
     for i in range(9):
         frame[i] = strain_in[i] + (1.0 if i % 4 == 0 else 0.0)
-
-    pl.semaphore_wait(barrier, around)
 
     lane = iota((8, 128), 1)
     sub = iota((8, 128), 0)
@@ -243,6 +243,10 @@
             send_low[step, p] = low
             send_high[step, p] = high
 
+        @pl.when(step == 0)
+        def _():
+            pl.semaphore_wait(barrier, around)
+
         for d, (dx, dy) in enumerate(DIRECTIONS):
 
             @pl.when(present(dx, dy))
@@ -385,14 +389,14 @@
     nx, ny = lax.axis_size("slope"), lax.axis_size("cross")
     f32 = jnp.float32
     vmem = pl.BlockSpec(memory_space=pltpu.VMEM)
-    smem = pl.BlockSpec(memory_space=pltpu.SMEM)
     hbm = pl.BlockSpec(memory_space=pltpu.HBM)
     outs = pl.pallas_call(
         functools.partial(kernel, nx, ny),
         out_shape=[jax.ShapeDtypeStruct((n, ROWS, 128), f32) for n in (3, 3, 9, 9)],
-        in_specs=[smem] + [hbm] * 6,
+        in_specs=[hbm] * 7,
         out_specs=[vmem] * 4,
         scratch_shapes=[
+            pltpu.SMEM((BLOCKS,), jnp.int32),
             pltpu.VMEM((9, ROWS, 128), f32),
             pltpu.VMEM((ROWS, 128), f32),
             pltpu.VMEM((ROWS, 128), f32),
@@ -414,7 +418,7 @@
             pltpu.VMEM((STEPS, 2, 8, 128), f32),
             pltpu.VMEM((STEPS, 2, 8, 128), f32),
             pltpu.VMEM((STEPS, 2, 8, 128), f32),
-            pltpu.SemaphoreType.DMA((6,)),
+            pltpu.SemaphoreType.DMA((7,)),
             pltpu.SemaphoreType.DMA((STEPS, 8)),
             pltpu.SemaphoreType.DMA((STEPS, 8)),
         ],
@@ -422,18 +426,23 @@
             collective_id=0, has_side_effects=True, vmem_limit_bytes=VMEM_BYTES
         ),
     )(
-        block_counts.reshape(BLOCKS),
-        offsets.reshape(3, ROWS, 128),
-        velocity.reshape(3, ROWS, 128),
-        affine.reshape(9, ROWS, 128),
-        strain.reshape(9, ROWS, 128),
-        particle_mass.reshape(ROWS, 128),
-        plastic_ratio.reshape(ROWS, 128),
+        *(
+            pltpu.with_memory_space_constraint(value, pltpu.HBM)
+            for value in (
+                block_counts.reshape(BLOCKS),
+                offsets.reshape(3, ROWS, 128),
+                velocity.reshape(3, ROWS, 128),
+                affine.reshape(9, ROWS, 128),
+                strain.reshape(9, ROWS, 128),
+                particle_mass.reshape(ROWS, 128),
+                plastic_ratio.reshape(ROWS, 128),
+            )
+        ),
     )
     outs = pl.pallas_call(
         write_out,
         out_shape=[jax.ShapeDtypeStruct(out.shape, f32) for out in outs],
-        in_specs=[hbm] * 4,
+        in_specs=[vmem] * 4,
         out_specs=[hbm] * 4,
         scratch_shapes=[pltpu.SemaphoreType.DMA((4,))],
         compiler_params=pltpu.CompilerParams(vmem_limit_bytes=VMEM_BYTES),

time: 58.4 us -> 44.4 us (0.76)
  Pallas kernels: 57.6 us -> 43.7 us
    pallas_call x1, Pallas kernels: 13.1 us -> 0.77 us  [per_device(): pl.pallas_call(write_out, out_shape=[jax.ShapeDtypeStruct(out.shape, f32)...]
    pallas_call x1, Pallas kernels: 44.6 us -> 42.9 us  [per_device(): pl.pallas_call(functools.partial(kernel, nx, ny), out_shape=[jax.ShapeDty...]
where the time goes in v1:
time: 44.4 us; the launch traced here: 44.3 us
  Pallas kernels  43.7 us (98%)
  between operations  0.64 us (1%)
    pallas_call x1, Pallas kernels, per_device(): pl.pallas_call(functools.partial(kernel, nx, ny), out_shape=[jax.ShapeDty...  42.9 us

profile of v1, /device:TPU:1, one launch (start us, length us, event | category | flops | bytes accessed | tf_op | source)
XLA Modules:
  0.0 44.3 jit_solution(6077297163500966703)
XLA Ops:
  0.6 42.9 %shard_map.102 = (f32[3,32,128]{2,1,0:T(8,128)S(1)}, f32[3,32,128]{2,1,0:T(8,128)S(1)}, f32[9,32,128]{2,1,0:T(8,128)S(1)}, f32[9,32,128]{2,1,0:T(8,128)S(1)}) custom-call(s32[8]{0:T(128)} %bitcast.17, f32[3,32,128]{2,1,0:T(8,128)} %bitcast.13, f32[3,32,128]{2,1,0:T(8,128)} %bitcast.14, f32[9,32,128]{2,1,0:T(8,128)} %bitcast.11, f32[9,32,128]{2,1,0:T(8,128)} %bitcast.12, ...), custom_call_target="tpu_custom_call" | custom-call | tf_op jit(solution)/shard_map/pallas_call | solution.py:393
  43.6 0.8 %shard_map.103 = (f32[3,32,128]{2,1,0:T(8,128)}, f32[3,32,128]{2,1,0:T(8,128)}, f32[9,32,128]{2,1,0:T(8,128)}, f32[9,32,128]{2,1,0:T(8,128)}) custom-call(f32[3,32,128]{2,1,0:T(8,128)S(1)} %get-tuple-element.12.off, f32[3,32,128]{2,1,0:T(8,128)S(1)} %get-tuple-element.13.vel, f32[9,32,128]{2,1,0:T(8,128)S(1)} %get-tuple-element.14.aff, ...), custom_call_target="tpu_custom_call" | custom-call | tf_op jit(solution)/shard_map/pallas_call | solution.py:442

commit v2 on v1

v2 whole, which is shorter than its diff:
```python
import functools

import jax
import jax.numpy as jnp
from jax import lax
from jax.experimental import pallas as pl
from jax.experimental.pallas import tpu as pltpu
from jax.sharding import PartitionSpec as P

STEPS = 5
BLOCKS = 8
ROWS = 32
CHUNKS = 4
TILES = 4
VMEM_BYTES = 40 * 1024 * 1024
MESH = pl.DeviceIdType.MESH

time_step = 0.02
shear_modulus = 4.0
lame_lambda = 4.0
hardening = 10.0
mass_floor = 0.25
gravity_slope = 1.5
gravity_vertical = -2.5
CENTRE = 2.5

DIRECTIONS = [(0, -1), (0, 1), (-1, -1), (-1, 1), (1, -1), (1, 1), (-1, 0), (1, 0)]


def iota(shape, dim):
    return lax.broadcasted_iota(jnp.int32, shape, dim)


def axis_weights(position):
    base = jnp.floor(position + 0.5)
    dist = position - base
    lower = 0.5 * (0.5 - dist) * (0.5 - dist)
    middle = 0.75 - dist * dist
    upper = 0.5 * (0.5 + dist) * (0.5 + dist)
    at = {e: base == float(e) for e in range(-1, 7)}
    return [
        jnp.where(at[e], middle, jnp.where(at[e + 1], lower, jnp.where(at[e - 1], upper, 0.0)))
        for e in range(6)
    ]


def split(values):
    high = values.astype(jnp.bfloat16)
    low = (values - high.astype(jnp.float32)).astype(jnp.bfloat16)
    return high, low


def kernel(
    nx, ny,
    counts_hbm, off_hbm, vel_hbm, aff_hbm, strain_hbm, mass_hbm, plastic_hbm,
    off, vel, aff, frame,
    counts, strain_in, mass_in, plastic_in, live_ref, mw_ref, hard_ref, wx, wy, wz, feats, bs, us,
    gathered, lower_speed, first_fields, spill_fields,
    send_x, send_low, send_high, recv_x, recv_low, recv_high, diag_low, diag_high,
    load_sem, send_sem, recv_sem,
):
    ix = lax.axis_index("slope")
    iy = lax.axis_index("cross")

    def neighbour(dx, dy):
        return (ix + dx + nx) % nx, (iy + dy + ny) % ny

    loads = [
        pltpu.make_async_copy(source, target, load_sem.at[i])
        for i, (source, target) in enumerate((
            (counts_hbm, counts), (mass_hbm, mass_in), (plastic_hbm, plastic_in), (off_hbm, off),
            (vel_hbm, vel), (aff_hbm, aff), (strain_hbm, strain_in),
        ))
    ]
    for load in loads:
        load.start()

    for ref in (recv_x, recv_low, recv_high, diag_low, diag_high):
        ref[...] = jnp.zeros(ref.shape, ref.dtype)
    barrier = pltpu.get_barrier_semaphore()
    for dx, dy in DIRECTIONS:
        pl.semaphore_signal(barrier, inc=1, device_id=neighbour(dx, dy), device_id_type=MESH)

    for ref in (wx, wz, us, bs, gathered):
        ref[...] = jnp.zeros(ref.shape, ref.dtype)
    for load in loads:
        load.wait()
    row = iota((ROWS, 128), 0)
    slot = (row % CHUNKS) * 128 + iota((ROWS, 128), 1)
    limit = jnp.zeros((ROWS, 128), jnp.int32)
    for k in range(BLOCKS):
        limit = jnp.where(row // CHUNKS == k, counts[k], limit)
    live = jnp.where(slot < limit, 1.0, 0.0).astype(jnp.float32)
    live_ref[...] = live
    mw_ref[...] = mass_in[...] * live
    hard_ref[...] = 4.0 * time_step * live * jnp.exp(hardening * (1.0 - plastic_in[...]))
    for i in range(9):
        frame[i] = strain_in[i] + (1.0 if i % 4 == 0 else 0.0)

    lane = iota((8, 128), 1)
    sub = iota((8, 128), 0)
    half = lane < 64
    r3 = lane % 8
    e2 = (lane % 64) // 8
    e3 = jnp.where(half, r3, (r3 + 4) % 8)
    ex = sub.astype(jnp.float32) - CENTRE
    ey = e2.astype(jnp.float32) - CENTRE
    ez = e3.astype(jnp.float32) - CENTRE
    own = half | (r3 >= 4)
    group = (lane % 64) // 16
    half80 = iota((80, 128), 1) < 64
    zero = jnp.zeros((8, 128), jnp.float32)
    place_x = 4 * ix + sub
    place_y = 4 * iy + e2
    inner_x = ((sub >= 2) | (ix > 0)) & ((sub < 4) | (ix < nx - 1))
    at_low = (group == 0) & (iy > 0)
    at_high = (group == 2) & (iy < ny - 1)
    outside = (place_x >= 4 * nx) | (place_y >= 4 * ny)

    def copy_to(step, p, d):
        dx, dy = DIRECTIONS[d]
        back = DIRECTIONS.index((-dx, -dy))
        if dy == 0:
            source, target = send_x.at[step, p], recv_x.at[step, p]
            source = source.at[:, pl.ds(0 if dx < 0 else 4, 2), :]
            target = target.at[:, pl.ds(4 if dx < 0 else 0, 2), :]
        else:
            if dx == 0:
                source, target = (send_low, recv_high) if dy < 0 else (send_high, recv_low)
                here, there = pl.ds(0, 6), pl.ds(0, 6)
            else:
                source, target = (send_low, diag_high) if dy < 0 else (send_high, diag_low)
                here, there = pl.ds(0 if dx < 0 else 4, 2), pl.ds(4 if dx < 0 else 0, 2)
            source, target = source.at[step, p, here, :], target.at[step, p, there, :]
        return pltpu.make_async_remote_copy(
            src_ref=source, dst_ref=target,
            send_sem=send_sem.at[step, p, d], recv_sem=recv_sem.at[step, p, back],
            device_id=neighbour(dx, dy), device_id_type=MESH,
        )

    def spread(ref, at):
        return jnp.broadcast_to(ref[pl.ds(at, 1), :], (8, 128))

    def terms(j, o, f, v, c):
        rows = pl.ds(8 * j, 8)
        det = (
            f[0] * (f[4] * f[8] - f[5] * f[7])
            - f[1] * (f[3] * f[8] - f[5] * f[6])
            + f[2] * (f[3] * f[7] - f[4] * f[6])
        )
        bulk = lame_lambda * (det - 1.0) * det
        mw = mw_ref[rows, :]
        hard = hard_ref[rows, :]
        terms_ = [[None] * 3 for _ in range(3)]
        for a in range(3):
            for b in range(a, 3):
                stretch = f[3 * a] * f[3 * b] + f[3 * a + 1] * f[3 * b + 1] + f[3 * a + 2] * f[3 * b + 2]
                if a == b:
                    tau = hard * (shear_modulus * (stretch - 1.0) + bulk)
                else:
                    tau = hard * (shear_modulus * stretch)
                terms_[a][b] = mw * c[3 * a + b] - tau
                if a != b:
                    terms_[b][a] = mw * c[3 * b + a] - tau
        feats[pl.ds(8 * j, 8), :] = mw
        for a in range(3):
            moved = (
                terms_[a][0] * (o[0] - CENTRE)
                + terms_[a][1] * (o[1] - CENTRE)
                + terms_[a][2] * (o[2] - CENTRE)
            )
            feats[pl.ds((1 + a) * ROWS + 8 * j, 8), :] = mw * v[a] - moved
            for b in range(3):
                feats[pl.ds((4 + 3 * b + a) * ROWS + 8 * j, 8), :] = terms_[a][b]
        for e, w in enumerate(axis_weights(o[0])):
            wx[pl.ds(e * ROWS + 8 * j, 8), :] = w
        for e, w in enumerate(axis_weights(o[1])):
            wy[pl.ds(e * ROWS + 8 * j, 8), :] = w
        for e, w in enumerate(axis_weights(o[2])):
            wz[pl.ds((4 + e) * ROWS + 8 * j, 8), :] = w
            if e >= 4:
                wz[pl.ds((e - 4) * ROWS + 8 * j, 8), :] = w

    def deposit(k):
        sides, planes = [], []
        for c in range(CHUNKS):
            r = CHUNKS * k + c
            wxs = wx[pl.ds(r, 8, stride=ROWS), :]
            wzs = wz[pl.ds(r + (4 * ROWS if k % 2 == 0 else 0), 8, stride=ROWS), :]
            planes.append(
                jnp.concatenate([spread(wy, e * ROWS + r) * wzs for e in range(6)], axis=0)
            )
            part = [spread(feats, i * ROWS + r) for i in range(13)]
            side = [part[0] * wxs]
            side += [(part[1 + a] + part[4 + a] * ex) * wxs for a in range(3)]
            side += [part[7 + i] * wxs for i in range(6)]
            sides.append(jnp.concatenate(side, axis=0))
        plane_high, plane_low = split(jnp.concatenate(planes, axis=1))
        bs[k, 0:48, :] = plane_high
        bs[k, 64:112, :] = plane_low
        side_high, side_low = split(jnp.concatenate(sides, axis=1))
        dots = lax.dot_general(
            jnp.concatenate([side_high, side_low], axis=0), bs[k],
            (((1,), (1,)), ((), ())), preferred_element_type=jnp.float32,
        )
        total = dots[:80] + dots[80:]
        return total + pltpu.roll(total, 64, 1)

    def deposit_tile(j):
        even, odd = deposit(2 * j), deposit(2 * j + 1)
        pair = [jnp.where(half, even[8 * i : 8 * i + 8], odd[8 * i : 8 * i + 8]) for i in range(10)]
        return [pair[0]] + [pair[1 + a] + ey * pair[4 + a] + ez * pair[7 + a] for a in range(3)]

    def send(step, p, before, first, second):
        low, high = zero, zero
        for i in range(4):
            one = jnp.where(own, first[i], before[i])
            two = jnp.where(own, second[i], first[i])
            mine = jnp.where(half, one, two) + pltpu.roll(jnp.where(half, two, one), 64, 1)
            send_x[step, p, i] = mine
            to_low = mine if i == 0 else pltpu.roll(mine, 16 * i, 1)
            shift = (16 * i - 32) % 128
            to_high = mine if shift == 0 else pltpu.roll(mine, shift, 1)
            low = jnp.where(group == i, to_low, low)
            high = jnp.where(group == i, to_high, high)
        send_low[step, p] = low
        send_high[step, p] = high

    def start(step, p):
        for d in range(8):
            copy_to(step, p, d).start()

    def arrive(step, p):
        for d in range(8):
            copy_to(step, p, d).wait_recv()

    def grid_speed(step, p):
        below = recv_low[step, p] + jnp.where(inner_x, diag_low[step, p], 0.0)
        above = recv_high[step, p] + jnp.where(inner_x, diag_high[step, p], 0.0)
        total = []
        for i in range(4):
            from_low = below if i == 0 else pltpu.roll(below, 128 - 16 * i, 1)
            shift = (32 - 16 * i) % 128
            from_high = above if shift == 0 else pltpu.roll(above, shift, 1)
            extra = jnp.where(at_low, from_low, jnp.where(at_high, from_high, 0.0))
            side = jnp.where(inner_x, recv_x[step, p, i], 0.0)
            total.append(send_x[step, p, i] + side + extra)
        scale = 1.0 / jnp.maximum(total[0], mass_floor)
        speed_x = total[1] * scale + time_step * gravity_slope
        speed_y = total[2] * scale
        speed_z = total[3] * scale + time_step * gravity_vertical
        place_z = 16 * p + jnp.where(half, 0, 8) + r3
        speed_x = jnp.where(place_x < 2, jnp.maximum(speed_x, 0.0), speed_x)
        speed_x = jnp.where(place_x >= 4 * nx - 2, jnp.minimum(speed_x, 0.0), speed_x)
        speed_y = jnp.where(place_y < 2, jnp.maximum(speed_y, 0.0), speed_y)
        speed_y = jnp.where(place_y >= 4 * ny - 2, jnp.minimum(speed_y, 0.0), speed_y)
        speed_z = jnp.where(place_z >= 8 * TILES - 2, jnp.minimum(speed_z, 0.0), speed_z)
        still = outside | (place_z < 2)
        return [jnp.where(still, 0.0, speed) for speed in (speed_x, speed_y, speed_z)]

    def windows(j, speed, turned, beyond):
        for a in range(3):
            if j % 2 == 0:
                window = jnp.where(half | (r3 < 4), speed[a], turned[a])
            else:
                window = jnp.where(half, turned[a], jnp.where(r3 >= 4, speed[a], beyond[a]))
            for b, factor in enumerate((None, ex, ey, ez)):
                q = 3 * b + a
                value = window if factor is None else window * factor
                if q < 8:
                    us[j, pl.ds(q, 6, stride=8), :] = value[:6]
                else:
                    us[j, pl.ds(48 + q - 8, 6, stride=4), :] = value[:6]

    def gather(k):
        both = us[k // 2]
        swapped = pltpu.roll(both, 64, 1)
        nodes = jnp.where(half80, both, swapped) if k % 2 == 0 else jnp.where(half80, swapped, both)
        left = jnp.concatenate(split(nodes), axis=1)
        planes = bs[k]
        taken = lax.dot_general(
            left, jnp.concatenate([planes, planes], axis=0),
            (((1,), (0,)), ((), ())), preferred_element_type=jnp.float32,
        )
        for c in range(CHUNKS):
            r = CHUNKS * k + c
            part = taken[:, 128 * c : 128 * c + 128]
            weights = [spread(wx, e * ROWS + r) for e in range(6)]
            first = weights[0] * part[0:8]
            for e in range(1, 6):
                first = first + weights[e] * part[8 * e : 8 * e + 8]
            second = jnp.where(sub < 4, weights[0], weights[1]) * part[48:56]
            for e in (2, 4):
                at = 48 + 4 * e
                second = second + jnp.where(sub < 4, weights[e], weights[e + 1]) * part[at : at + 8]
            gathered[pl.ds(16 * r, 8), :] = first
            gathered[pl.ds(16 * r + 8, 8), :] = second

    def advance(j):
        rows = pl.ds(8 * j, 8)

        def quantity(q):
            value = gathered[pl.ds(128 * j + q, 8, stride=16), :]
            if q >= 8:
                value = value + gathered[pl.ds(128 * j + q + 4, 8, stride=16), :]
            return value

        o = [off[i, rows, :] for i in range(3)]
        f = [frame[i, rows, :] for i in range(9)]
        v = [quantity(a) for a in range(3)]
        c = [None] * 9
        for a in range(3):
            for b in range(3):
                c[3 * a + b] = 4.0 * (quantity(3 + 3 * b + a) - v[a] * (o[b] - CENTRE))
        o = [o[a] + time_step * v[a] for a in range(3)]
        f = [
            f[3 * a + b]
            + time_step * (c[3 * a] * f[b] + c[3 * a + 1] * f[3 + b] + c[3 * a + 2] * f[6 + b])
            for a in range(3)
            for b in range(3)
        ]
        for ref, values in ((off, o), (vel, v), (aff, c), (frame, f)):
            for i, value in enumerate(values):
                ref[i, rows, :] = value
        return o, f, v, c

    def keep(ref, values):
        for i, value in enumerate(values):
            ref[i] = value

    def turn(values):
        return [pltpu.roll(value, 64, 1) for value in values]

    def phases(step, go_on):
        arrive(step, 0)
        speed = grid_speed(step, 0)
        turned = turn(speed)
        keep(lower_speed, speed)
        windows(0, speed, turned, None)
        windows(1, speed, turned, [zero] * 3)
        for k in range(3):
            gather(k)
        state = advance(0)
        if go_on:
            terms(0, *state)
            keep(first_fields, deposit_tile(0))

        arrive(step, 1)
        upper = grid_speed(step, 1)
        upper_turned = turn(upper)
        speed = [lower_speed[a] for a in range(3)]
        windows(1, speed, turn(speed), upper_turned)
        gather(3)
        state = advance(1)
        if go_on:
            terms(1, *state)
            fields = deposit_tile(1)
            keep(spill_fields, fields)
            send(step + 1, 0, [zero] * 4, [first_fields[i] for i in range(4)], fields)
            start(step + 1, 0)

        windows(2, upper, upper_turned, None)
        windows(3, upper, upper_turned, [zero] * 3)
        for k in range(4, 8):
            gather(k)
        states = [advance(2), advance(3)]
        if go_on:
            terms(2, *states[0])
            terms(3, *states[1])
            fields = [deposit_tile(2), deposit_tile(3)]
            send(step + 1, 1, [spill_fields[i] for i in range(4)], *fields)
            start(step + 1, 1)

    for j in range(TILES):
        rows = pl.ds(8 * j, 8)
        terms(j, *([ref[i, rows, :] for i in range(n)] for ref, n in ((off, 3), (frame, 9), (vel, 3), (aff, 9))))
    fields = [deposit_tile(0), deposit_tile(1)]
    send(0, 0, [zero] * 4, *fields)
    pl.semaphore_wait(barrier, 8)
    start(0, 0)
    before = fields[1]
    fields = [deposit_tile(2), deposit_tile(3)]
    send(0, 1, before, *fields)
    start(0, 1)

    def one_step(step, carry):
        phases(step, True)
        return carry

    lax.fori_loop(0, STEPS - 1, one_step, 0)
    phases(STEPS - 1, False)

    def finish(step, carry):
        for p in range(2):
            for d in range(8):
                copy_to(step, p, d).wait_send()
        return carry

    lax.fori_loop(0, STEPS, finish, 0)
    live = live_ref[...]
    for ref, count in ((off, 3), (vel, 3), (aff, 9), (frame, 9)):
        for i in range(count):
            ref[i] = ref[i] * live


def write_out(off, vel, aff, frame, off_out, vel_out, aff_out, frame_out, sem):
    copies = [
        pltpu.make_async_copy(source, target, sem.at[i])
        for i, (source, target) in enumerate(
            ((aff, aff_out), (frame, frame_out), (off, off_out), (vel, vel_out))
        )
    ]
    for copy in copies:
        copy.start()
    for copy in copies:
        copy.wait()


def per_device(offsets, velocity, affine, strain, particle_mass, plastic_ratio, block_counts):
    nx, ny = lax.axis_size("slope"), lax.axis_size("cross")
    f32 = jnp.float32
    vmem = pl.BlockSpec(memory_space=pltpu.VMEM)
    hbm = pl.BlockSpec(memory_space=pltpu.HBM)
    outs = pl.pallas_call(
        functools.partial(kernel, nx, ny),
        out_shape=[jax.ShapeDtypeStruct((n, ROWS, 128), f32) for n in (3, 3, 9, 9)],
        in_specs=[hbm] * 7,
        out_specs=[vmem] * 4,
        scratch_shapes=[
            pltpu.SMEM((BLOCKS,), jnp.int32),
            pltpu.VMEM((9, ROWS, 128), f32),
            pltpu.VMEM((ROWS, 128), f32),
            pltpu.VMEM((ROWS, 128), f32),
            pltpu.VMEM((ROWS, 128), f32),
            pltpu.VMEM((ROWS, 128), f32),
            pltpu.VMEM((ROWS, 128), f32),
            pltpu.VMEM((8 * ROWS, 128), f32),
            pltpu.VMEM((6 * ROWS, 128), f32),
            pltpu.VMEM((12 * ROWS, 128), f32),
            pltpu.VMEM((13 * ROWS, 128), f32),
            pltpu.VMEM((BLOCKS, 128, 512), jnp.bfloat16),
            pltpu.VMEM((TILES, 80, 128), f32),
            pltpu.VMEM((16 * ROWS, 128), f32),
            pltpu.VMEM((3, 8, 128), f32),
            pltpu.VMEM((4, 8, 128), f32),
            pltpu.VMEM((4, 8, 128), f32),
            pltpu.VMEM((STEPS, 2, 4, 8, 128), f32),
            pltpu.VMEM((STEPS, 2, 8, 128), f32),
            pltpu.VMEM((STEPS, 2, 8, 128), f32),
            pltpu.VMEM((STEPS, 2, 4, 8, 128), f32),
            pltpu.VMEM((STEPS, 2, 8, 128), f32),
            pltpu.VMEM((STEPS, 2, 8, 128), f32),
            pltpu.VMEM((STEPS, 2, 8, 128), f32),
            pltpu.VMEM((STEPS, 2, 8, 128), f32),
            pltpu.SemaphoreType.DMA((7,)),
            pltpu.SemaphoreType.DMA((STEPS, 2, 8)),
            pltpu.SemaphoreType.DMA((STEPS, 2, 8)),
        ],
        compiler_params=pltpu.CompilerParams(
            collective_id=0, has_side_effects=True, vmem_limit_bytes=VMEM_BYTES
        ),
    )(
        *(
            pltpu.with_memory_space_constraint(value, pltpu.HBM)
            for value in (
                block_counts.reshape(BLOCKS),
                offsets.reshape(3, ROWS, 128),
                velocity.reshape(3, ROWS, 128),
                affine.reshape(9, ROWS, 128),
                strain.reshape(9, ROWS, 128),
                particle_mass.reshape(ROWS, 128),
                plastic_ratio.reshape(ROWS, 128),
            )
        ),
    )
    outs = pl.pallas_call(
        write_out,
        out_shape=[jax.ShapeDtypeStruct(out.shape, f32) for out in outs],
        in_specs=[vmem] * 4,
        out_specs=[hbm] * 4,
        scratch_shapes=[pltpu.SemaphoreType.DMA((4,))],
        compiler_params=pltpu.CompilerParams(vmem_limit_bytes=VMEM_BYTES),
    )(*outs)
    return tuple(out.reshape(out.shape[0], 1, 1, ROWS * 128) for out in outs)


def solution(mesh):
    wide = P(None, "slope", "cross", None)
    flat = P("slope", "cross", None)
    return jax.shard_map(
        per_device,
        mesh=mesh,
        in_specs=(wide, wide, wide, wide, flat, flat, flat),
        out_specs=(wide, wide, wide, wide),
        check_vma=False,
    )
```

time: 44.4 us -> 51.8 us (1.17)
  Pallas kernels: 43.7 us -> 51 us
    pallas_call x1, Pallas kernels: 42.9 us -> 50.2 us  [per_device(): pl.pallas_call(functools.partial(kernel, nx, ny), out_shape=[jax.ShapeDty...]
where the time goes in v2:
time: 51.8 us; the launch traced here: 51.6 us
  Pallas kernels  51 us (98%)
  between operations  0.64 us (1%)
    pallas_call x1, Pallas kernels, per_device(): pl.pallas_call(functools.partial(kernel, nx, ny), out_shape=[jax.ShapeDty...  50.2 us

profile of v2, /device:TPU:1, one launch (start us, length us, event | category | flops | bytes accessed | tf_op | source)
XLA Modules:
  0.0 51.6 jit_solution(8296114053538688715)
XLA Ops:
  0.6 50.2 %shard_map.102 = (f32[3,32,128]{2,1,0:T(8,128)S(1)}, f32[3,32,128]{2,1,0:T(8,128)S(1)}, f32[9,32,128]{2,1,0:T(8,128)S(1)}, f32[9,32,128]{2,1,0:T(8,128)S(1)}) custom-call(s32[8]{0:T(128)} %bitcast.17, f32[3,32,128]{2,1,0:T(8,128)} %bitcast.13, f32[3,32,128]{2,1,0:T(8,128)} %bitcast.14, f32[9,32,128]{2,1,0:T(8,128)} %bitcast.11, f32[9,32,128]{2,1,0:T(8,128)} %bitcast.12, ...), custom_call_target="tpu_custom_call" | custom-call | tf_op jit(solution)/shard_map/pallas_call | solution.py:424
  50.9 0.8 %shard_map.103 = (f32[3,32,128]{2,1,0:T(8,128)}, f32[3,32,128]{2,1,0:T(8,128)}, f32[9,32,128]{2,1,0:T(8,128)}, f32[9,32,128]{2,1,0:T(8,128)}) custom-call(f32[3,32,128]{2,1,0:T(8,128)S(1)} %get-tuple-element.12.off, f32[3,32,128]{2,1,0:T(8,128)S(1)} %get-tuple-element.13.vel, f32[9,32,128]{2,1,0:T(8,128)S(1)} %get-tuple-element.14.aff, ...), custom_call_target="tpu_custom_call" | custom-call | tf_op jit(solution)/shard_map/pallas_call | solution.py:476

commit v3 on v2

--- a/solution.py
+++ b/solution.py
@@ -54,8 +54,8 @@
     nx, ny,
     counts_hbm, off_hbm, vel_hbm, aff_hbm, strain_hbm, mass_hbm, plastic_hbm,
     off, vel, aff, frame,
-    counts, strain_in, mass_in, plastic_in, live_ref, mw_ref, hard_ref, wx, wy, wz, feats, bs, us,
-    gathered, lower_speed, first_fields, spill_fields,
+    counts, strain_in, mass_in, plastic_in, live_ref, mw_ref, hard_ref, wx, wy, wz, feats, bs, sides, us,
+    gathered,
     send_x, send_low, send_high, recv_x, recv_low, recv_high, diag_low, diag_high,
     load_sem, send_sem, recv_sem,
 ):
@@ -63,7 +63,31 @@
     iy = lax.axis_index("cross")
 
     def neighbour(dx, dy):
-        return (ix + dx + nx) % nx, (iy + dy + ny) % ny
+        return ix + dx, iy + dy
+
+    def present(dx, dy):
+        ok = None
+        for d, i, n in ((dx, ix, nx), (dy, iy, ny)):
+            if d != 0:
+                here = (i + d >= 0) & (i + d < n)
+                ok = here if ok is None else ok & here
+        return ok
+
+    inside = (ix > 0) & (ix < nx - 1) & (iy > 0) & (iy < ny - 1)
+
+    def each_neighbour(act):
+        @pl.when(inside)
+        def _():
+            for d in range(8):
+                act(d)
+
+        @pl.when(jnp.logical_not(inside))
+        def _():
+            for d, (dx, dy) in enumerate(DIRECTIONS):
+
+                @pl.when(present(dx, dy))
+                def _():
+                    act(d)
 
     loads = [
         pltpu.make_async_copy(source, target, load_sem.at[i])
@@ -78,8 +102,14 @@
     for ref in (recv_x, recv_low, recv_high, diag_low, diag_high):
         ref[...] = jnp.zeros(ref.shape, ref.dtype)
     barrier = pltpu.get_barrier_semaphore()
+    around = jnp.int32(0)
     for dx, dy in DIRECTIONS:
-        pl.semaphore_signal(barrier, inc=1, device_id=neighbour(dx, dy), device_id_type=MESH)
+        ok = present(dx, dy)
+        around = around + jnp.where(ok, 1, 0).astype(jnp.int32)
+
+        @pl.when(ok)
+        def _():
+            pl.semaphore_signal(barrier, inc=1, device_id=neighbour(dx, dy), device_id_type=MESH)
 
     for ref in (wx, wz, us, bs, gathered):
         ref[...] = jnp.zeros(ref.shape, ref.dtype)
@@ -108,33 +138,30 @@
     ez = e3.astype(jnp.float32) - CENTRE
     own = half | (r3 >= 4)
     group = (lane % 64) // 16
-    half80 = iota((80, 128), 1) < 64
+    own_tile = half == (r3 >= 4)
+    ez_even = r3.astype(jnp.float32) - CENTRE
+    ez_odd = ((r3 + 4) % 8).astype(jnp.float32) - CENTRE
     zero = jnp.zeros((8, 128), jnp.float32)
     place_x = 4 * ix + sub
     place_y = 4 * iy + e2
-    inner_x = ((sub >= 2) | (ix > 0)) & ((sub < 4) | (ix < nx - 1))
-    at_low = (group == 0) & (iy > 0)
-    at_high = (group == 2) & (iy < ny - 1)
     outside = (place_x >= 4 * nx) | (place_y >= 4 * ny)
 
-    def copy_to(step, p, d):
+    def copy_to(step, d):
         dx, dy = DIRECTIONS[d]
         back = DIRECTIONS.index((-dx, -dy))
         if dy == 0:
-            source, target = send_x.at[step, p], recv_x.at[step, p]
-            source = source.at[:, pl.ds(0 if dx < 0 else 4, 2), :]
-            target = target.at[:, pl.ds(4 if dx < 0 else 0, 2), :]
+            source, target = send_x, recv_x
+        elif dx == 0:
+            source, target = (send_low, recv_high) if dy < 0 else (send_high, recv_low)
         else:
-            if dx == 0:
-                source, target = (send_low, recv_high) if dy < 0 else (send_high, recv_low)
-                here, there = pl.ds(0, 6), pl.ds(0, 6)
-            else:
-                source, target = (send_low, diag_high) if dy < 0 else (send_high, diag_low)
-                here, there = pl.ds(0 if dx < 0 else 4, 2), pl.ds(4 if dx < 0 else 0, 2)
-            source, target = source.at[step, p, here, :], target.at[step, p, there, :]
+            source, target = (send_low, diag_high) if dy < 0 else (send_high, diag_low)
+        if dx == 0:
+            here, there = pl.ds(0, 6), pl.ds(0, 6)
+        else:
+            here, there = pl.ds(0 if dx < 0 else 4, 2), pl.ds(4 if dx < 0 else 0, 2)
         return pltpu.make_async_remote_copy(
-            src_ref=source, dst_ref=target,
-            send_sem=send_sem.at[step, p, d], recv_sem=recv_sem.at[step, p, back],
+            src_ref=source.at[step, :, here, :], dst_ref=target.at[step, :, there, :],
+            send_sem=send_sem.at[step, d], recv_sem=recv_sem.at[step, back],
             device_id=neighbour(dx, dy), device_id_type=MESH,
         )
 
@@ -182,33 +209,36 @@
                 wz[pl.ds((e - 4) * ROWS + 8 * j, 8), :] = w
 
     def deposit(k):
-        sides, planes = [], []
         for c in range(CHUNKS):
             r = CHUNKS * k + c
+            lanes = pl.ds(128 * c, 128)
             wxs = wx[pl.ds(r, 8, stride=ROWS), :]
             wzs = wz[pl.ds(r + (4 * ROWS if k % 2 == 0 else 0), 8, stride=ROWS), :]
-            planes.append(
-                jnp.concatenate([spread(wy, e * ROWS + r) * wzs for e in range(6)], axis=0)
-            )
+            for e in (0, 2, 4):
+                high, low = split(jnp.concatenate(
+                    [spread(wy, e * ROWS + r) * wzs, spread(wy, (e + 1) * ROWS + r) * wzs], axis=0
+                ))
+                bs[k, pl.ds(8 * e, 16), lanes] = high
+                bs[k, pl.ds(64 + 8 * e, 16), lanes] = low
             part = [spread(feats, i * ROWS + r) for i in range(13)]
             side = [part[0] * wxs]
             side += [(part[1 + a] + part[4 + a] * ex) * wxs for a in range(3)]
             side += [part[7 + i] * wxs for i in range(6)]
-            sides.append(jnp.concatenate(side, axis=0))
-        plane_high, plane_low = split(jnp.concatenate(planes, axis=1))
-        bs[k, 0:48, :] = plane_high
-        bs[k, 64:112, :] = plane_low
-        side_high, side_low = split(jnp.concatenate(sides, axis=1))
+            for i in range(0, 10, 2):
+                high, low = split(jnp.concatenate(side[i : i + 2], axis=0))
+                sides[k, pl.ds(8 * i, 16), lanes] = high
+                sides[k, pl.ds(80 + 8 * i, 16), lanes] = low
         dots = lax.dot_general(
-            jnp.concatenate([side_high, side_low], axis=0), bs[k],
-            (((1,), (1,)), ((), ())), preferred_element_type=jnp.float32,
-        )
-        total = dots[:80] + dots[80:]
-        return total + pltpu.roll(total, 64, 1)
+            sides[k], bs[k], (((1,), (1,)), ((), ())), preferred_element_type=jnp.float32
+        )
+        return dots[:80] + dots[80:]
 
     def deposit_tile(j):
         even, odd = deposit(2 * j), deposit(2 * j + 1)
-        pair = [jnp.where(half, even[8 * i : 8 * i + 8], odd[8 * i : 8 * i + 8]) for i in range(10)]
+        pair = []
+        for i in range(10):
+            one, two = even[8 * i : 8 * i + 8], odd[8 * i : 8 * i + 8]
+            pair.append(jnp.where(half, one, two) + pltpu.roll(jnp.where(half, two, one), 64, 1))
         return [pair[0]] + [pair[1 + a] + ey * pair[4 + a] + ez * pair[7 + a] for a in range(3)]
 
     def send(step, p, before, first, second):
@@ -217,7 +247,7 @@
             one = jnp.where(own, first[i], before[i])
             two = jnp.where(own, second[i], first[i])
             mine = jnp.where(half, one, two) + pltpu.roll(jnp.where(half, two, one), 64, 1)
-            send_x[step, p, i] = mine
+            send_x[step, 4 * p + i] = mine
             to_low = mine if i == 0 else pltpu.roll(mine, 16 * i, 1)
             shift = (16 * i - 32) % 128
             to_high = mine if shift == 0 else pltpu.roll(mine, shift, 1)
@@ -226,25 +256,16 @@
         send_low[step, p] = low
         send_high[step, p] = high
 
-    def start(step, p):
-        for d in range(8):
-            copy_to(step, p, d).start()
-
-    def arrive(step, p):
-        for d in range(8):
-            copy_to(step, p, d).wait_recv()
-
     def grid_speed(step, p):
-        below = recv_low[step, p] + jnp.where(inner_x, diag_low[step, p], 0.0)
-        above = recv_high[step, p] + jnp.where(inner_x, diag_high[step, p], 0.0)
+        below = recv_low[step, p] + diag_low[step, p]
+        above = recv_high[step, p] + diag_high[step, p]
         total = []
         for i in range(4):
             from_low = below if i == 0 else pltpu.roll(below, 128 - 16 * i, 1)
             shift = (32 - 16 * i) % 128
             from_high = above if shift == 0 else pltpu.roll(above, shift, 1)
-            extra = jnp.where(at_low, from_low, jnp.where(at_high, from_high, 0.0))
-            side = jnp.where(inner_x, recv_x[step, p, i], 0.0)
-            total.append(send_x[step, p, i] + side + extra)
+            extra = jnp.where(group == 0, from_low, jnp.where(group == 2, from_high, 0.0))
+            total.append(send_x[step, 4 * p + i] + recv_x[step, 4 * p + i] + extra)
         scale = 1.0 / jnp.maximum(total[0], mass_floor)
         speed_x = total[1] * scale + time_step * gravity_slope
         speed_y = total[2] * scale
@@ -258,25 +279,31 @@
         still = outside | (place_z < 2)
         return [jnp.where(still, 0.0, speed) for speed in (speed_x, speed_y, speed_z)]
 
-    def windows(j, speed, turned, beyond):
+    def windows(k, speed, turned, beyond, beyond_turned):
         for a in range(3):
-            if j % 2 == 0:
-                window = jnp.where(half | (r3 < 4), speed[a], turned[a])
+            first, second = (speed[a], turned[a]) if k % 4 < 2 else (turned[a], speed[a])
+            if k % 2 == 0:
+                window = jnp.where(half, first, second)
+            elif k % 4 == 1:
+                window = jnp.where(own_tile, first, second)
             else:
-                window = jnp.where(half, turned[a], jnp.where(r3 >= 4, speed[a], beyond[a]))
-            for b, factor in enumerate((None, ex, ey, ez)):
+                window = jnp.where(
+                    r3 >= 4,
+                    jnp.where(half, first, second),
+                    jnp.where(half, beyond[a], beyond_turned[a]),
+                )
+            for b, factor in enumerate((None, ex, ey, ez_odd if k % 2 else ez_even)):
                 q = 3 * b + a
                 value = window if factor is None else window * factor
                 if q < 8:
-                    us[j, pl.ds(q, 6, stride=8), :] = value[:6]
+                    us[k, pl.ds(q, 8, stride=8), :] = value
                 else:
-                    us[j, pl.ds(48 + q - 8, 6, stride=4), :] = value[:6]
+                    us[k, pl.ds(64 + q - 8, 8, stride=4), :] = value
 
     def gather(k):
-        both = us[k // 2]
-        swapped = pltpu.roll(both, 64, 1)
-        nodes = jnp.where(half80, both, swapped) if k % 2 == 0 else jnp.where(half80, swapped, both)
-        left = jnp.concatenate(split(nodes), axis=1)
+        left = jnp.concatenate(
+            split(jnp.concatenate([us[k, 0:48, :], us[k, 64:96, :]], axis=0)), axis=1
+        )
         planes = bs[k]
         taken = lax.dot_general(
             left, jnp.concatenate([planes, planes], axis=0),
@@ -324,76 +351,43 @@
                 ref[i, rows, :] = value
         return o, f, v, c
 
-    def keep(ref, values):
-        for i, value in enumerate(values):
-            ref[i] = value
-
     def turn(values):
         return [pltpu.roll(value, 64, 1) for value in values]
 
-    def phases(step, go_on):
-        arrive(step, 0)
-        speed = grid_speed(step, 0)
-        turned = turn(speed)
-        keep(lower_speed, speed)
-        windows(0, speed, turned, None)
-        windows(1, speed, turned, [zero] * 3)
-        for k in range(3):
+    def one_step(step, carry):
+        fields = [deposit_tile(j) for j in range(TILES)]
+        send(step, 0, [zero] * 4, fields[0], fields[1])
+        send(step, 1, fields[1], fields[2], fields[3])
+
+        @pl.when(step == 0)
+        def _():
+            pl.semaphore_wait(barrier, around)
+
+        each_neighbour(lambda d: copy_to(step, d).start())
+
+        def wait(d):
+            dx, dy = DIRECTIONS[d]
+            copy_to(step, DIRECTIONS.index((-dx, -dy))).wait_recv()
+
+        each_neighbour(wait)
+        speed = [grid_speed(step, p) for p in range(2)] + [[zero] * 3]
+        turned = [turn(speed[0]), turn(speed[1]), [zero] * 3]
+        for k in range(BLOCKS):
+            p = k // 4
+            windows(k, speed[p], turned[p], speed[p + 1], turned[p + 1])
+        for k in range(BLOCKS):
             gather(k)
-        state = advance(0)
-        if go_on:
-            terms(0, *state)
-            keep(first_fields, deposit_tile(0))
-
-        arrive(step, 1)
-        upper = grid_speed(step, 1)
-        upper_turned = turn(upper)
-        speed = [lower_speed[a] for a in range(3)]
-        windows(1, speed, turn(speed), upper_turned)
-        gather(3)
-        state = advance(1)
-        if go_on:
-            terms(1, *state)
-            fields = deposit_tile(1)
-            keep(spill_fields, fields)
-            send(step + 1, 0, [zero] * 4, [first_fields[i] for i in range(4)], fields)
-            start(step + 1, 0)
-
-        windows(2, upper, upper_turned, None)
-        windows(3, upper, upper_turned, [zero] * 3)
-        for k in range(4, 8):
-            gather(k)
-        states = [advance(2), advance(3)]
-        if go_on:
-            terms(2, *states[0])
-            terms(3, *states[1])
-            fields = [deposit_tile(2), deposit_tile(3)]
-            send(step + 1, 1, [spill_fields[i] for i in range(4)], *fields)
-            start(step + 1, 1)
+        for j in range(TILES):
+            terms(j, *advance(j))
+        return carry
 
     for j in range(TILES):
         rows = pl.ds(8 * j, 8)
         terms(j, *([ref[i, rows, :] for i in range(n)] for ref, n in ((off, 3), (frame, 9), (vel, 3), (aff, 9))))
-    fields = [deposit_tile(0), deposit_tile(1)]
-    send(0, 0, [zero] * 4, *fields)
-    pl.semaphore_wait(barrier, 8)
-    start(0, 0)
-    before = fields[1]
-    fields = [deposit_tile(2), deposit_tile(3)]
-    send(0, 1, before, *fields)
-    start(0, 1)
-
-    def one_step(step, carry):
-        phases(step, True)
-        return carry
-
-    lax.fori_loop(0, STEPS - 1, one_step, 0)
-    phases(STEPS - 1, False)
+    lax.fori_loop(0, STEPS, one_step, 0)
 
     def finish(step, carry):
-        for p in range(2):
-            for d in range(8):
-                copy_to(step, p, d).wait_send()
+        each_neighbour(lambda d: copy_to(step, d).wait_send())
         return carry
 
     lax.fori_loop(0, STEPS, finish, 0)
@@ -439,22 +433,20 @@
             pltpu.VMEM((12 * ROWS, 128), f32),
             pltpu.VMEM((13 * ROWS, 128), f32),
             pltpu.VMEM((BLOCKS, 128, 512), jnp.bfloat16),
-            pltpu.VMEM((TILES, 80, 128), f32),
+            pltpu.VMEM((BLOCKS, 160, 512), jnp.bfloat16),
+            pltpu.VMEM((BLOCKS, 96, 128), f32),
             pltpu.VMEM((16 * ROWS, 128), f32),
-            pltpu.VMEM((3, 8, 128), f32),
-            pltpu.VMEM((4, 8, 128), f32),
-            pltpu.VMEM((4, 8, 128), f32),
-            pltpu.VMEM((STEPS, 2, 4, 8, 128), f32),
-            pltpu.VMEM((STEPS, 2, 8, 128), f32),
-            pltpu.VMEM((STEPS, 2, 8, 128), f32),
-            pltpu.VMEM((STEPS, 2, 4, 8, 128), f32),
+            pltpu.VMEM((STEPS, 8, 8, 128), f32),
+            pltpu.VMEM((STEPS, 2, 8, 128), f32),
+            pltpu.VMEM((STEPS, 2, 8, 128), f32),
+            pltpu.VMEM((STEPS, 8, 8, 128), f32),
             pltpu.VMEM((STEPS, 2, 8, 128), f32),
             pltpu.VMEM((STEPS, 2, 8, 128), f32),
             pltpu.VMEM((STEPS, 2, 8, 128), f32),
             pltpu.VMEM((STEPS, 2, 8, 128), f32),
             pltpu.SemaphoreType.DMA((7,)),
-            pltpu.SemaphoreType.DMA((STEPS, 2, 8)),
-            pltpu.SemaphoreType.DMA((STEPS, 2, 8)),
+            pltpu.SemaphoreType.DMA((STEPS, 8)),
+            pltpu.SemaphoreType.DMA((STEPS, 8)),
         ],
         compiler_params=pltpu.CompilerParams(
             collective_id=0, has_side_effects=True, vmem_limit_bytes=VMEM_BYTES

time: 51.8 us -> 44.8 us (0.86)
  Pallas kernels: 51 us -> 44.1 us
    pallas_call x1, Pallas kernels: 50.2 us -> 43.3 us  [per_device(): pl.pallas_call(functools.partial(kernel, nx, ny), out_shape=[jax.ShapeDty...]
where the time goes in v3:
time: 44.8 us; the launch traced here: 44.7 us
  Pallas kernels  44.1 us (98%)
  between operations  0.64 us (1%)
    pallas_call x1, Pallas kernels, per_device(): pl.pallas_call(functools.partial(kernel, nx, ny), out_shape=[jax.ShapeDty...  43.3 us

profile of v3, /device:TPU:1, one launch (start us, length us, event | category | flops | bytes accessed | tf_op | source)
XLA Modules:
  0.0 44.7 jit_solution(18023771369165289066)
XLA Ops:
  0.6 43.3 %shard_map.102 = (f32[3,32,128]{2,1,0:T(8,128)S(1)}, f32[3,32,128]{2,1,0:T(8,128)S(1)}, f32[9,32,128]{2,1,0:T(8,128)S(1)}, f32[9,32,128]{2,1,0:T(8,128)S(1)}) custom-call(s32[8]{0:T(128)} %bitcast.17, f32[3,32,128]{2,1,0:T(8,128)} %bitcast.13, f32[3,32,128]{2,1,0:T(8,128)} %bitcast.14, f32[9,32,128]{2,1,0:T(8,128)} %bitcast.11, f32[9,32,128]{2,1,0:T(8,128)} %bitcast.12, ...), custom_call_target="tpu_custom_call" | custom-call | tf_op jit(solution)/shard_map/pallas_call | solution.py:418
  43.9 0.8 %shard_map.103 = (f32[3,32,128]{2,1,0:T(8,128)}, f32[3,32,128]{2,1,0:T(8,128)}, f32[9,32,128]{2,1,0:T(8,128)}, f32[9,32,128]{2,1,0:T(8,128)}) custom-call(f32[3,32,128]{2,1,0:T(8,128)S(1)} %get-tuple-element.12.off, f32[3,32,128]{2,1,0:T(8,128)S(1)} %get-tuple-element.13.vel, f32[9,32,128]{2,1,0:T(8,128)S(1)} %get-tuple-element.14.aff, ...), custom_call_target="tpu_custom_call" | custom-call | tf_op jit(solution)/shard_map/pallas_call | solution.py:468

commit v4 on v3

--- a/solution.py
+++ b/solution.py
@@ -302,13 +302,12 @@
 
     def gather(k):
         left = jnp.concatenate(
-            split(jnp.concatenate([us[k, 0:48, :], us[k, 64:96, :]], axis=0)), axis=1
-        )
-        planes = bs[k]
+            split(jnp.concatenate([us[k, 0:48, :], us[k, 64:96, :]], axis=0)), axis=0
+        )
         taken = lax.dot_general(
-            left, jnp.concatenate([planes, planes], axis=0),
-            (((1,), (0,)), ((), ())), preferred_element_type=jnp.float32,
-        )
+            left, bs[k], (((1,), (0,)), ((), ())), preferred_element_type=jnp.float32
+        )
+        taken = taken[:80] + taken[80:]
         for c in range(CHUNKS):
             r = CHUNKS * k + c
             part = taken[:, 128 * c : 128 * c + 128]
@@ -355,6 +354,9 @@
         return [pltpu.roll(value, 64, 1) for value in values]
 
     def one_step(step, carry):
+        for j in range(TILES):
+            rows = pl.ds(8 * j, 8)
+            terms(j, *([ref[i, rows, :] for i in range(n)] for ref, n in ((off, 3), (frame, 9), (vel, 3), (aff, 9))))
         fields = [deposit_tile(j) for j in range(TILES)]
         send(step, 0, [zero] * 4, fields[0], fields[1])
         send(step, 1, fields[1], fields[2], fields[3])
@@ -378,12 +380,9 @@
         for k in range(BLOCKS):
             gather(k)
         for j in range(TILES):
-            terms(j, *advance(j))
+            advance(j)
         return carry
 
-    for j in range(TILES):
-        rows = pl.ds(8 * j, 8)
-        terms(j, *([ref[i, rows, :] for i in range(n)] for ref, n in ((off, 3), (frame, 9), (vel, 3), (aff, 9))))
     lax.fori_loop(0, STEPS, one_step, 0)
 
     def finish(step, carry):

time: 44.8 us -> 44.8 us (level)
  no operation moved by 1% of the time
where the time goes in v4:
time: 44.8 us; the launch traced here: 44.7 us
  Pallas kernels  44.1 us (98%)
  between operations  0.64 us (1%)
    pallas_call x1, Pallas kernels, per_device(): pl.pallas_call(functools.partial(kernel, nx, ny), out_shape=[jax.ShapeDty...  43.3 us

profile of v4, /device:TPU:1, one launch (start us, length us, event | category | flops | bytes accessed | tf_op | source)
XLA Modules:
  0.0 44.7 jit_solution(2214702314003571929)
XLA Ops:
  0.6 43.3 %shard_map.102 = (f32[3,32,128]{2,1,0:T(8,128)S(1)}, f32[3,32,128]{2,1,0:T(8,128)S(1)}, f32[9,32,128]{2,1,0:T(8,128)S(1)}, f32[9,32,128]{2,1,0:T(8,128)S(1)}) custom-call(s32[8]{0:T(128)} %bitcast.17, f32[3,32,128]{2,1,0:T(8,128)} %bitcast.13, f32[3,32,128]{2,1,0:T(8,128)} %bitcast.14, f32[9,32,128]{2,1,0:T(8,128)} %bitcast.11, f32[9,32,128]{2,1,0:T(8,128)} %bitcast.12, ...), custom_call_target="tpu_custom_call" | custom-call | tf_op jit(solution)/shard_map/pallas_call | solution.py:417
  44.0 0.8 %shard_map.103 = (f32[3,32,128]{2,1,0:T(8,128)}, f32[3,32,128]{2,1,0:T(8,128)}, f32[9,32,128]{2,1,0:T(8,128)}, f32[9,32,128]{2,1,0:T(8,128)}) custom-call(f32[3,32,128]{2,1,0:T(8,128)S(1)} %get-tuple-element.12.off, f32[3,32,128]{2,1,0:T(8,128)S(1)} %get-tuple-element.13.vel, f32[9,32,128]{2,1,0:T(8,128)S(1)} %get-tuple-element.14.aff, ...), custom_call_target="tpu_custom_call" | custom-call | tf_op jit(solution)/shard_map/pallas_call | solution.py:467

commit v5 on v4

--- a/solution.py
+++ b/solution.py
@@ -146,7 +146,7 @@
     place_y = 4 * iy + e2
     outside = (place_x >= 4 * nx) | (place_y >= 4 * ny)
 
-    def copy_to(step, d):
+    def copy_to(step, p, d):
         dx, dy = DIRECTIONS[d]
         back = DIRECTIONS.index((-dx, -dy))
         if dy == 0:
@@ -160,8 +160,8 @@
         else:
             here, there = pl.ds(0 if dx < 0 else 4, 2), pl.ds(4 if dx < 0 else 0, 2)
         return pltpu.make_async_remote_copy(
-            src_ref=source.at[step, :, here, :], dst_ref=target.at[step, :, there, :],
-            send_sem=send_sem.at[step, d], recv_sem=recv_sem.at[step, back],
+            src_ref=source.at[step, p, :, here, :], dst_ref=target.at[step, p, :, there, :],
+            send_sem=send_sem.at[step, p, d], recv_sem=recv_sem.at[step, p, back],
             device_id=neighbour(dx, dy), device_id_type=MESH,
         )
 
@@ -247,25 +247,25 @@
             one = jnp.where(own, first[i], before[i])
             two = jnp.where(own, second[i], first[i])
             mine = jnp.where(half, one, two) + pltpu.roll(jnp.where(half, two, one), 64, 1)
-            send_x[step, 4 * p + i] = mine
+            send_x[step, p, i] = mine
             to_low = mine if i == 0 else pltpu.roll(mine, 16 * i, 1)
             shift = (16 * i - 32) % 128
             to_high = mine if shift == 0 else pltpu.roll(mine, shift, 1)
             low = jnp.where(group == i, to_low, low)
             high = jnp.where(group == i, to_high, high)
-        send_low[step, p] = low
-        send_high[step, p] = high
+        send_low[step, p, 0] = low
+        send_high[step, p, 0] = high
 
     def grid_speed(step, p):
-        below = recv_low[step, p] + diag_low[step, p]
-        above = recv_high[step, p] + diag_high[step, p]
+        below = recv_low[step, p, 0] + diag_low[step, p, 0]
+        above = recv_high[step, p, 0] + diag_high[step, p, 0]
         total = []
         for i in range(4):
             from_low = below if i == 0 else pltpu.roll(below, 128 - 16 * i, 1)
             shift = (32 - 16 * i) % 128
             from_high = above if shift == 0 else pltpu.roll(above, shift, 1)
             extra = jnp.where(group == 0, from_low, jnp.where(group == 2, from_high, 0.0))
-            total.append(send_x[step, 4 * p + i] + recv_x[step, 4 * p + i] + extra)
+            total.append(send_x[step, p, i] + recv_x[step, p, i] + extra)
         scale = 1.0 / jnp.maximum(total[0], mass_floor)
         speed_x = total[1] * scale + time_step * gravity_slope
         speed_y = total[2] * scale
@@ -357,19 +357,22 @@
         for j in range(TILES):
             rows = pl.ds(8 * j, 8)
             terms(j, *([ref[i, rows, :] for i in range(n)] for ref, n in ((off, 3), (frame, 9), (vel, 3), (aff, 9))))
-        fields = [deposit_tile(j) for j in range(TILES)]
+        fields = [deposit_tile(0), deposit_tile(1)]
         send(step, 0, [zero] * 4, fields[0], fields[1])
-        send(step, 1, fields[1], fields[2], fields[3])
 
         @pl.when(step == 0)
         def _():
             pl.semaphore_wait(barrier, around)
 
-        each_neighbour(lambda d: copy_to(step, d).start())
+        each_neighbour(lambda d: copy_to(step, 0, d).start())
+        fields += [deposit_tile(2), deposit_tile(3)]
+        send(step, 1, fields[1], fields[2], fields[3])
+        each_neighbour(lambda d: copy_to(step, 1, d).start())
 
         def wait(d):
             dx, dy = DIRECTIONS[d]
-            copy_to(step, DIRECTIONS.index((-dx, -dy))).wait_recv()
+            for p in range(2):
+                copy_to(step, p, DIRECTIONS.index((-dx, -dy))).wait_recv()
 
         each_neighbour(wait)
         speed = [grid_speed(step, p) for p in range(2)] + [[zero] * 3]
@@ -386,7 +389,8 @@
     lax.fori_loop(0, STEPS, one_step, 0)
 
     def finish(step, carry):
-        each_neighbour(lambda d: copy_to(step, d).wait_send())
+        for p in range(2):
+            each_neighbour(lambda d: copy_to(step, p, d).wait_send())
         return carry
 
     lax.fori_loop(0, STEPS, finish, 0)
@@ -435,17 +439,17 @@
             pltpu.VMEM((BLOCKS, 160, 512), jnp.bfloat16),
             pltpu.VMEM((BLOCKS, 96, 128), f32),
             pltpu.VMEM((16 * ROWS, 128), f32),
-            pltpu.VMEM((STEPS, 8, 8, 128), f32),
-            pltpu.VMEM((STEPS, 2, 8, 128), f32),
-            pltpu.VMEM((STEPS, 2, 8, 128), f32),
-            pltpu.VMEM((STEPS, 8, 8, 128), f32),
-            pltpu.VMEM((STEPS, 2, 8, 128), f32),
-            pltpu.VMEM((STEPS, 2, 8, 128), f32),
-            pltpu.VMEM((STEPS, 2, 8, 128), f32),
-            pltpu.VMEM((STEPS, 2, 8, 128), f32),
+            pltpu.VMEM((STEPS, 2, 4, 8, 128), f32),
+            pltpu.VMEM((STEPS, 2, 1, 8, 128), f32),
+            pltpu.VMEM((STEPS, 2, 1, 8, 128), f32),
+            pltpu.VMEM((STEPS, 2, 4, 8, 128), f32),
+            pltpu.VMEM((STEPS, 2, 1, 8, 128), f32),
+            pltpu.VMEM((STEPS, 2, 1, 8, 128), f32),
+            pltpu.VMEM((STEPS, 2, 1, 8, 128), f32),
+            pltpu.VMEM((STEPS, 2, 1, 8, 128), f32),
             pltpu.SemaphoreType.DMA((7,)),
-            pltpu.SemaphoreType.DMA((STEPS, 8)),
-            pltpu.SemaphoreType.DMA((STEPS, 8)),
+            pltpu.SemaphoreType.DMA((STEPS, 2, 8)),
+            pltpu.SemaphoreType.DMA((STEPS, 2, 8)),
         ],
         compiler_params=pltpu.CompilerParams(
             collective_id=0, has_side_effects=True, vmem_limit_bytes=VMEM_BYTES

time: 44.8 us -> 46.9 us (1.047)
  Pallas kernels: 44.1 us -> 46.1 us
    pallas_call x1, Pallas kernels: 43.3 us -> 45.4 us  [per_device(): pl.pallas_call(functools.partial(kernel, nx, ny), out_shape=[jax.ShapeDty...]
where the time goes in v5:
time: 46.9 us; the launch traced here: 46.8 us
  Pallas kernels  46.1 us (98%)
  between operations  0.64 us (1%)
    pallas_call x1, Pallas kernels, per_device(): pl.pallas_call(functools.partial(kernel, nx, ny), out_shape=[jax.ShapeDty...  45.4 us

profile of v5, /device:TPU:1, one launch (start us, length us, event | category | flops | bytes accessed | tf_op | source)
XLA Modules:
  0.0 46.8 jit_solution(13442712031421953646)
XLA Ops:
  0.6 45.4 %shard_map.102 = (f32[3,32,128]{2,1,0:T(8,128)S(1)}, f32[3,32,128]{2,1,0:T(8,128)S(1)}, f32[9,32,128]{2,1,0:T(8,128)S(1)}, f32[9,32,128]{2,1,0:T(8,128)S(1)}) custom-call(s32[8]{0:T(128)} %bitcast.17, f32[3,32,128]{2,1,0:T(8,128)} %bitcast.13, f32[3,32,128]{2,1,0:T(8,128)} %bitcast.14, f32[9,32,128]{2,1,0:T(8,128)} %bitcast.11, f32[9,32,128]{2,1,0:T(8,128)} %bitcast.12, ...), custom_call_target="tpu_custom_call" | custom-call | tf_op jit(solution)/shard_map/pallas_call | solution.py:421
  46.0 0.8 %shard_map.103 = (f32[3,32,128]{2,1,0:T(8,128)}, f32[3,32,128]{2,1,0:T(8,128)}, f32[9,32,128]{2,1,0:T(8,128)}, f32[9,32,128]{2,1,0:T(8,128)}) custom-call(f32[3,32,128]{2,1,0:T(8,128)S(1)} %get-tuple-element.12.off, f32[3,32,128]{2,1,0:T(8,128)S(1)} %get-tuple-element.13.vel, f32[9,32,128]{2,1,0:T(8,128)S(1)} %get-tuple-element.14.aff, ...), custom_call_target="tpu_custom_call" | custom-call | tf_op jit(solution)/shard_map/pallas_call | solution.py:471

commit v6 on v4

--- a/solution.py
+++ b/solution.py
@@ -55,7 +55,7 @@
     counts_hbm, off_hbm, vel_hbm, aff_hbm, strain_hbm, mass_hbm, plastic_hbm,
     off, vel, aff, frame,
     counts, strain_in, mass_in, plastic_in, live_ref, mw_ref, hard_ref, wx, wy, wz, feats, bs, sides, us,
-    gathered,
+    gathered, counted,
     send_x, send_low, send_high, recv_x, recv_low, recv_high, diag_low, diag_high,
     load_sem, send_sem, recv_sem,
 ):
@@ -148,7 +148,6 @@
 
     def copy_to(step, d):
         dx, dy = DIRECTIONS[d]
-        back = DIRECTIONS.index((-dx, -dy))
         if dy == 0:
             source, target = send_x, recv_x
         elif dx == 0:
@@ -161,9 +160,21 @@
             here, there = pl.ds(0 if dx < 0 else 4, 2), pl.ds(4 if dx < 0 else 0, 2)
         return pltpu.make_async_remote_copy(
             src_ref=source.at[step, :, here, :], dst_ref=target.at[step, :, there, :],
-            send_sem=send_sem.at[step, d], recv_sem=recv_sem.at[step, back],
+            send_sem=send_sem, recv_sem=recv_sem.at[step],
             device_id=neighbour(dx, dy), device_id_type=MESH,
         )
+
+    def passed(sem, rows):
+        pltpu.make_async_copy(counted.at[pl.ds(0, rows), :], counted.at[pl.ds(0, rows), :], sem).wait()
+
+    def each_edge(act):
+        side_x = (ix == 0) | (ix == nx - 1)
+        side_y = (iy == 0) | (iy == ny - 1)
+        for at_x, at_y, rows in ((0, 0, 72), (1, 0, 48), (0, 1, 52), (1, 1, 32)):
+
+            @pl.when((side_x == bool(at_x)) & (side_y == bool(at_y)))
+            def _():
+                act(rows)
 
     def spread(ref, at):
         return jnp.broadcast_to(ref[pl.ds(at, 1), :], (8, 128))
@@ -367,11 +378,7 @@
 
         each_neighbour(lambda d: copy_to(step, d).start())
 
-        def wait(d):
-            dx, dy = DIRECTIONS[d]
-            copy_to(step, DIRECTIONS.index((-dx, -dy))).wait_recv()
-
-        each_neighbour(wait)
+        each_edge(lambda rows: passed(recv_sem.at[step], rows))
         speed = [grid_speed(step, p) for p in range(2)] + [[zero] * 3]
         turned = [turn(speed[0]), turn(speed[1]), [zero] * 3]
         for k in range(BLOCKS):
@@ -385,11 +392,7 @@
 
     lax.fori_loop(0, STEPS, one_step, 0)
 
-    def finish(step, carry):
-        each_neighbour(lambda d: copy_to(step, d).wait_send())
-        return carry
-
-    lax.fori_loop(0, STEPS, finish, 0)
+    each_edge(lambda rows: passed(send_sem, STEPS * rows))
     live = live_ref[...]
     for ref, count in ((off, 3), (vel, 3), (aff, 9), (frame, 9)):
         for i in range(count):
@@ -435,6 +438,7 @@
             pltpu.VMEM((BLOCKS, 160, 512), jnp.bfloat16),
             pltpu.VMEM((BLOCKS, 96, 128), f32),
             pltpu.VMEM((16 * ROWS, 128), f32),
+            pltpu.VMEM((STEPS * 72, 128), f32),
             pltpu.VMEM((STEPS, 8, 8, 128), f32),
             pltpu.VMEM((STEPS, 2, 8, 128), f32),
             pltpu.VMEM((STEPS, 2, 8, 128), f32),
@@ -444,8 +448,8 @@
             pltpu.VMEM((STEPS, 2, 8, 128), f32),
             pltpu.VMEM((STEPS, 2, 8, 128), f32),
             pltpu.SemaphoreType.DMA((7,)),
-            pltpu.SemaphoreType.DMA((STEPS, 8)),
-            pltpu.SemaphoreType.DMA((STEPS, 8)),
+            pltpu.SemaphoreType.DMA,
+            pltpu.SemaphoreType.DMA((STEPS,)),
         ],
         compiler_params=pltpu.CompilerParams(
             collective_id=0, has_side_effects=True, vmem_limit_bytes=VMEM_BYTES

time: 44.8 us -> 44 us (0.982)
  Pallas kernels: 44.1 us -> 43.3 us
    pallas_call x1, Pallas kernels: 43.3 us -> 42.5 us  [per_device(): pl.pallas_call(functools.partial(kernel, nx, ny), out_shape=[jax.ShapeDty...]
where the time goes in v6:
time: 44 us; the launch traced here: 43.9 us
  Pallas kernels  43.3 us (98%)
  between operations  0.64 us (1%)
    pallas_call x1, Pallas kernels, per_device(): pl.pallas_call(functools.partial(kernel, nx, ny), out_shape=[jax.ShapeDty...  42.5 us

profile of v6, /device:TPU:1, one launch (start us, length us, event | category | flops | bytes accessed | tf_op | source)
XLA Modules:
  0.0 43.9 jit_solution(17721398970586556384)
XLA Ops:
  0.6 42.5 %shard_map.102 = (f32[3,32,128]{2,1,0:T(8,128)S(1)}, f32[3,32,128]{2,1,0:T(8,128)S(1)}, f32[9,32,128]{2,1,0:T(8,128)S(1)}, f32[9,32,128]{2,1,0:T(8,128)S(1)}) custom-call(s32[8]{0:T(128)} %bitcast.17, f32[3,32,128]{2,1,0:T(8,128)} %bitcast.13, f32[3,32,128]{2,1,0:T(8,128)} %bitcast.14, f32[9,32,128]{2,1,0:T(8,128)} %bitcast.11, f32[9,32,128]{2,1,0:T(8,128)} %bitcast.12, ...), custom_call_target="tpu_custom_call" | custom-call | tf_op jit(solution)/shard_map/pallas_call | solution.py:420
  43.2 0.8 %shard_map.103 = (f32[3,32,128]{2,1,0:T(8,128)}, f32[3,32,128]{2,1,0:T(8,128)}, f32[9,32,128]{2,1,0:T(8,128)}, f32[9,32,128]{2,1,0:T(8,128)}) custom-call(f32[3,32,128]{2,1,0:T(8,128)S(1)} %get-tuple-element.12.off, f32[3,32,128]{2,1,0:T(8,128)S(1)} %get-tuple-element.13.vel, f32[9,32,128]{2,1,0:T(8,128)S(1)} %get-tuple-element.14.aff, ...), custom_call_target="tpu_custom_call" | custom-call | tf_op jit(solution)/shard_map/pallas_call | solution.py:471

commit v7 on v6

--- a/solution.py
+++ b/solution.py
@@ -54,7 +54,7 @@
     nx, ny,
     counts_hbm, off_hbm, vel_hbm, aff_hbm, strain_hbm, mass_hbm, plastic_hbm,
     off, vel, aff, frame,
-    counts, strain_in, mass_in, plastic_in, live_ref, mw_ref, hard_ref, wx, wy, wz, feats, bs, sides, us,
+    counts, strain_in, mass_in, plastic_in, live_ref, mw_ref, hard_ref, wx, side_rows, plane_rows, pairs, bs, sides, us,
     gathered, counted,
     send_x, send_low, send_high, recv_x, recv_low, recv_high, diag_low, diag_high,
     load_sem, send_sem, recv_sem,
@@ -111,7 +111,7 @@
         def _():
             pl.semaphore_signal(barrier, inc=1, device_id=neighbour(dx, dy), device_id_type=MESH)
 
-    for ref in (wx, wz, us, bs, gathered):
+    for ref in (side_rows, plane_rows, us, bs):
         ref[...] = jnp.zeros(ref.shape, ref.dtype)
     for load in loads:
         load.wait()
@@ -176,11 +176,11 @@
             def _():
                 act(rows)
 
-    def spread(ref, at):
-        return jnp.broadcast_to(ref[pl.ds(at, 1), :], (8, 128))
-
-    def terms(j, o, f, v, c):
+    def terms(j):
         rows = pl.ds(8 * j, 8)
+        o, f, v, c = (
+            [ref[i, rows, :] for i in range(n)] for ref, n in ((off, 3), (frame, 9), (vel, 3), (aff, 9))
+        )
         det = (
             f[0] * (f[4] * f[8] - f[5] * f[7])
             - f[1] * (f[3] * f[8] - f[5] * f[6])
@@ -189,7 +189,7 @@
         bulk = lame_lambda * (det - 1.0) * det
         mw = mw_ref[rows, :]
         hard = hard_ref[rows, :]
-        terms_ = [[None] * 3 for _ in range(3)]
+        pull = [[None] * 3 for _ in range(3)]
         for a in range(3):
             for b in range(a, 3):
                 stretch = f[3 * a] * f[3 * b] + f[3 * a + 1] * f[3 * b + 1] + f[3 * a + 2] * f[3 * b + 2]
@@ -197,59 +197,54 @@
                     tau = hard * (shear_modulus * (stretch - 1.0) + bulk)
                 else:
                     tau = hard * (shear_modulus * stretch)
-                terms_[a][b] = mw * c[3 * a + b] - tau
+                pull[a][b] = mw * c[3 * a + b] - tau
                 if a != b:
-                    terms_[b][a] = mw * c[3 * b + a] - tau
-        feats[pl.ds(8 * j, 8), :] = mw
+                    pull[b][a] = mw * c[3 * b + a] - tau
+        push = []
         for a in range(3):
             moved = (
-                terms_[a][0] * (o[0] - CENTRE)
-                + terms_[a][1] * (o[1] - CENTRE)
-                + terms_[a][2] * (o[2] - CENTRE)
+                pull[a][0] * (o[0] - CENTRE) + pull[a][1] * (o[1] - CENTRE) + pull[a][2] * (o[2] - CENTRE)
             )
-            feats[pl.ds((1 + a) * ROWS + 8 * j, 8), :] = mw * v[a] - moved
-            for b in range(3):
-                feats[pl.ds((4 + 3 * b + a) * ROWS + 8 * j, 8), :] = terms_[a][b]
-        for e, w in enumerate(axis_weights(o[0])):
-            wx[pl.ds(e * ROWS + 8 * j, 8), :] = w
-        for e, w in enumerate(axis_weights(o[1])):
-            wy[pl.ds(e * ROWS + 8 * j, 8), :] = w
-        for e, w in enumerate(axis_weights(o[2])):
-            wz[pl.ds((4 + e) * ROWS + 8 * j, 8), :] = w
-            if e >= 4:
-                wz[pl.ds((e - 4) * ROWS + 8 * j, 8), :] = w
-
-    def deposit(k):
-        for c in range(CHUNKS):
-            r = CHUNKS * k + c
-            lanes = pl.ds(128 * c, 128)
-            wxs = wx[pl.ds(r, 8, stride=ROWS), :]
-            wzs = wz[pl.ds(r + (4 * ROWS if k % 2 == 0 else 0), 8, stride=ROWS), :]
-            for e in (0, 2, 4):
-                high, low = split(jnp.concatenate(
-                    [spread(wy, e * ROWS + r) * wzs, spread(wy, (e + 1) * ROWS + r) * wzs], axis=0
-                ))
-                bs[k, pl.ds(8 * e, 16), lanes] = high
-                bs[k, pl.ds(64 + 8 * e, 16), lanes] = low
-            part = [spread(feats, i * ROWS + r) for i in range(13)]
-            side = [part[0] * wxs]
-            side += [(part[1 + a] + part[4 + a] * ex) * wxs for a in range(3)]
-            side += [part[7 + i] * wxs for i in range(6)]
-            for i in range(0, 10, 2):
-                high, low = split(jnp.concatenate(side[i : i + 2], axis=0))
-                sides[k, pl.ds(8 * i, 16), lanes] = high
-                sides[k, pl.ds(80 + 8 * i, 16), lanes] = low
-        dots = lax.dot_general(
-            sides[k], bs[k], (((1,), (1,)), ((), ())), preferred_element_type=jnp.float32
-        )
-        return dots[:80] + dots[80:]
+            push.append(mw * v[a] - moved)
+        return mw, push, pull, [axis_weights(o[i]) for i in range(3)]
 
     def deposit_tile(j):
-        even, odd = deposit(2 * j), deposit(2 * j + 1)
-        pair = []
-        for i in range(10):
-            one, two = even[8 * i : 8 * i + 8], odd[8 * i : 8 * i + 8]
-            pair.append(jnp.where(half, one, two) + pltpu.roll(jnp.where(half, two, one), 64, 1))
+        mw, push, pull, weights = terms(j)
+        for e in range(6):
+            at = weights[0][e]
+            wx[j, e] = at
+            side = [mw]
+            side += [push[a] + (e - CENTRE) * pull[a][0] for a in range(3)]
+            side += [pull[a][b] for b in (1, 2) for a in range(3)]
+            for i, value in enumerate(side):
+                side_rows[j, pl.ds(8 * (6 * i + e), 8), :] = value * at
+        for e in range(6):
+            for z in range(6):
+                value = weights[1][e] * weights[2][z]
+                plane_rows[j, 0, pl.ds(8 * (8 * e + z), 8), :] = value
+                plane_rows[j, 1, pl.ds(8 * (8 * e + (z + 4) % 8), 8), :] = value
+        totals = []
+        for odd in range(2):
+            k = 2 * j + odd
+            for c in range(CHUNKS):
+                s = CHUNKS * odd + c
+                lanes = pl.ds(128 * c, 128)
+                high, low = split(plane_rows[j, odd, pl.ds(s, 48, stride=8), :])
+                bs[k, 0:48, lanes] = high
+                bs[k, 64:112, lanes] = low
+                high, low = split(side_rows[j, pl.ds(s, 64, stride=8), :])
+                sides[k, 0:64, lanes] = high
+                sides[k, 64:128, lanes] = low
+            dots = lax.dot_general(
+                sides[k], bs[k], (((1,), (1,)), ((), ())), preferred_element_type=jnp.float32
+            )
+            totals.append(dots[:64] + dots[64:])
+        for i in range(8):
+            one, two = totals[0][8 * i : 8 * i + 8], totals[1][8 * i : 8 * i + 8]
+            pairs[j, pl.ds(8 * i, 8), :] = jnp.where(half, one, two) + pltpu.roll(
+                jnp.where(half, two, one), 64, 1
+            )
+        pair = [pairs[j, pl.ds(6 * i, 8), :] for i in range(10)]
         return [pair[0]] + [pair[1 + a] + ey * pair[4 + a] + ez * pair[7 + a] for a in range(3)]
 
     def send(step, p, before, first, second):
@@ -306,40 +301,27 @@
             for b, factor in enumerate((None, ex, ey, ez_odd if k % 2 else ez_even)):
                 q = 3 * b + a
                 value = window if factor is None else window * factor
-                if q < 8:
-                    us[k, pl.ds(q, 8, stride=8), :] = value
-                else:
-                    us[k, pl.ds(64 + q - 8, 8, stride=4), :] = value
+                us[k, pl.ds(q, 8, stride=12), :] = value
 
     def gather(k):
-        left = jnp.concatenate(
-            split(jnp.concatenate([us[k, 0:48, :], us[k, 64:96, :]], axis=0)), axis=0
+        left = jnp.concatenate(split(us[k, 0:80, :]), axis=1)
+        planes = bs[k]
+        taken = lax.dot_general(
+            left, jnp.concatenate([planes, planes], axis=0),
+            (((1,), (0,)), ((), ())), preferred_element_type=jnp.float32,
         )
-        taken = lax.dot_general(
-            left, bs[k], (((1,), (0,)), ((), ())), preferred_element_type=jnp.float32
-        )
-        taken = taken[:80] + taken[80:]
         for c in range(CHUNKS):
-            r = CHUNKS * k + c
-            part = taken[:, 128 * c : 128 * c + 128]
-            weights = [spread(wx, e * ROWS + r) for e in range(6)]
-            first = weights[0] * part[0:8]
-            for e in range(1, 6):
-                first = first + weights[e] * part[8 * e : 8 * e + 8]
-            second = jnp.where(sub < 4, weights[0], weights[1]) * part[48:56]
-            for e in (2, 4):
-                at = 48 + 4 * e
-                second = second + jnp.where(sub < 4, weights[e], weights[e + 1]) * part[at : at + 8]
-            gathered[pl.ds(16 * r, 8), :] = first
-            gathered[pl.ds(16 * r + 8, 8), :] = second
+            s = CHUNKS * (k % 2) + c
+            gathered[k // 2, pl.ds(s, 72, stride=8), :] = taken[:72, 128 * c : 128 * c + 128]
 
     def advance(j):
         rows = pl.ds(8 * j, 8)
+        weights = [wx[j, e] for e in range(6)]
 
         def quantity(q):
-            value = gathered[pl.ds(128 * j + q, 8, stride=16), :]
-            if q >= 8:
-                value = value + gathered[pl.ds(128 * j + q + 4, 8, stride=16), :]
+            value = weights[0] * gathered[j, pl.ds(8 * q, 8), :]
+            for e in range(1, 6):
+                value = value + weights[e] * gathered[j, pl.ds(8 * (12 * e + q), 8), :]
             return value
 
         o = [off[i, rows, :] for i in range(3)]
@@ -365,9 +347,6 @@
         return [pltpu.roll(value, 64, 1) for value in values]
 
     def one_step(step, carry):
-        for j in range(TILES):
-            rows = pl.ds(8 * j, 8)
-            terms(j, *([ref[i, rows, :] for i in range(n)] for ref, n in ((off, 3), (frame, 9), (vel, 3), (aff, 9))))
         fields = [deposit_tile(j) for j in range(TILES)]
         send(step, 0, [zero] * 4, fields[0], fields[1])
         send(step, 1, fields[1], fields[2], fields[3])
@@ -430,14 +409,14 @@
             pltpu.VMEM((ROWS, 128), f32),
             pltpu.VMEM((ROWS, 128), f32),
             pltpu.VMEM((ROWS, 128), f32),
-            pltpu.VMEM((8 * ROWS, 128), f32),
-            pltpu.VMEM((6 * ROWS, 128), f32),
-            pltpu.VMEM((12 * ROWS, 128), f32),
-            pltpu.VMEM((13 * ROWS, 128), f32),
+            pltpu.VMEM((TILES, 6, 8, 128), f32),
+            pltpu.VMEM((TILES, 512, 128), f32),
+            pltpu.VMEM((TILES, 2, 384, 128), f32),
+            pltpu.VMEM((TILES, 64, 128), f32),
             pltpu.VMEM((BLOCKS, 128, 512), jnp.bfloat16),
-            pltpu.VMEM((BLOCKS, 160, 512), jnp.bfloat16),
+            pltpu.VMEM((BLOCKS, 128, 512), jnp.bfloat16),
             pltpu.VMEM((BLOCKS, 96, 128), f32),
-            pltpu.VMEM((16 * ROWS, 128), f32),
+            pltpu.VMEM((TILES, 576, 128), f32),
             pltpu.VMEM((STEPS * 72, 128), f32),
             pltpu.VMEM((STEPS, 8, 8, 128), f32),
             pltpu.VMEM((STEPS, 2, 8, 128), f32),

time: 44 us -> 44 us (level)
  no operation moved by 1% of the time
where the time goes in v7:
time: 44 us; the launch traced here: 43.9 us
  Pallas kernels  43.2 us (98%)
  between operations  0.64 us (1%)
    pallas_call x1, Pallas kernels, per_device(): pl.pallas_call(functools.partial(kernel, nx, ny), out_shape=[jax.ShapeDty...  42.5 us

profile of v7, /device:TPU:1, one launch (start us, length us, event | category | flops | bytes accessed | tf_op | source)
XLA Modules:
  0.0 43.9 jit_solution(14464198135370221833)
XLA Ops:
  0.6 42.5 %shard_map.102 = (f32[3,32,128]{2,1,0:T(8,128)S(1)}, f32[3,32,128]{2,1,0:T(8,128)S(1)}, f32[9,32,128]{2,1,0:T(8,128)S(1)}, f32[9,32,128]{2,1,0:T(8,128)S(1)}) custom-call(s32[8]{0:T(128)} %bitcast.17, f32[3,32,128]{2,1,0:T(8,128)} %bitcast.13, f32[3,32,128]{2,1,0:T(8,128)} %bitcast.14, f32[9,32,128]{2,1,0:T(8,128)} %bitcast.11, f32[9,32,128]{2,1,0:T(8,128)} %bitcast.12, ...), custom_call_target="tpu_custom_call" | custom-call | tf_op jit(solution)/shard_map/pallas_call | solution.py:399
  43.1 0.8 %shard_map.103 = (f32[3,32,128]{2,1,0:T(8,128)}, f32[3,32,128]{2,1,0:T(8,128)}, f32[9,32,128]{2,1,0:T(8,128)}, f32[9,32,128]{2,1,0:T(8,128)}) custom-call(f32[3,32,128]{2,1,0:T(8,128)S(1)} %get-tuple-element.12.off, f32[3,32,128]{2,1,0:T(8,128)S(1)} %get-tuple-element.13.vel, f32[9,32,128]{2,1,0:T(8,128)S(1)} %get-tuple-element.14.aff, ...), custom_call_target="tpu_custom_call" | custom-call | tf_op jit(solution)/shard_map/pallas_call | solution.py:450

commit v8 on v7

--- a/solution.py
+++ b/solution.py
@@ -24,7 +24,7 @@
 gravity_vertical = -2.5
 CENTRE = 2.5
 
-DIRECTIONS = [(0, -1), (0, 1), (-1, -1), (-1, 1), (1, -1), (1, 1), (-1, 0), (1, 0)]
+DIRECTIONS = [(-1, -1), (1, 1), (-1, 1), (1, -1), (0, -1), (0, 1), (-1, 0), (1, 0)]
 
 
 def iota(shape, dim):
@@ -96,9 +96,6 @@
             (vel_hbm, vel), (aff_hbm, aff), (strain_hbm, strain_in),
         ))
     ]
-    for load in loads:
-        load.start()
-
     for ref in (recv_x, recv_low, recv_high, diag_low, diag_high):
         ref[...] = jnp.zeros(ref.shape, ref.dtype)
     barrier = pltpu.get_barrier_semaphore()
@@ -111,6 +108,8 @@
         def _():
             pl.semaphore_signal(barrier, inc=1, device_id=neighbour(dx, dy), device_id_type=MESH)
 
+    for load in loads:
+        load.start()
     for ref in (side_rows, plane_rows, us, bs):
         ref[...] = jnp.zeros(ref.shape, ref.dtype)
     for load in loads:
@@ -247,16 +246,19 @@
         pair = [pairs[j, pl.ds(6 * i, 8), :] for i in range(10)]
         return [pair[0]] + [pair[1 + a] + ey * pair[4 + a] + ez * pair[7 + a] for a in range(3)]
 
+    def turned_sum(near, far, shift):
+        kept = near if shift == 0 else pltpu.roll(near, shift % 128, 1)
+        return kept + pltpu.roll(far, (shift + 64) % 128, 1)
+
     def send(step, p, before, first, second):
         low, high = zero, zero
         for i in range(4):
             one = jnp.where(own, first[i], before[i])
             two = jnp.where(own, second[i], first[i])
-            mine = jnp.where(half, one, two) + pltpu.roll(jnp.where(half, two, one), 64, 1)
-            send_x[step, 4 * p + i] = mine
-            to_low = mine if i == 0 else pltpu.roll(mine, 16 * i, 1)
-            shift = (16 * i - 32) % 128
-            to_high = mine if shift == 0 else pltpu.roll(mine, shift, 1)
+            near, far = jnp.where(half, one, two), jnp.where(half, two, one)
+            send_x[step, 4 * p + i] = turned_sum(near, far, 0)
+            to_low = turned_sum(near, far, 16 * i)
+            to_high = turned_sum(near, far, 16 * i - 32)
             low = jnp.where(group == i, to_low, low)
             high = jnp.where(group == i, to_high, high)
         send_low[step, p] = low
@@ -314,7 +316,7 @@
             s = CHUNKS * (k % 2) + c
             gathered[k // 2, pl.ds(s, 72, stride=8), :] = taken[:72, 128 * c : 128 * c + 128]
 
-    def advance(j):
+    def advance(j, last):
         rows = pl.ds(8 * j, 8)
         weights = [wx[j, e] for e in range(6)]
 
@@ -338,44 +340,48 @@
             for a in range(3)
             for b in range(3)
         ]
+        live_now = live_ref[rows, :]
         for ref, values in ((off, o), (vel, v), (aff, c), (frame, f)):
             for i, value in enumerate(values):
-                ref[i, rows, :] = value
-        return o, f, v, c
+                ref[i, rows, :] = value * live_now if last else value
 
     def turn(values):
         return [pltpu.roll(value, 64, 1) for value in values]
 
-    def one_step(step, carry):
-        fields = [deposit_tile(j) for j in range(TILES)]
+    def send_all(step, fields):
         send(step, 0, [zero] * 4, fields[0], fields[1])
         send(step, 1, fields[1], fields[2], fields[3])
 
-        @pl.when(step == 0)
-        def _():
-            pl.semaphore_wait(barrier, around)
-
+    def start_all(step):
         each_neighbour(lambda d: copy_to(step, d).start())
 
+    def take(step, last):
         each_edge(lambda rows: passed(recv_sem.at[step], rows))
         speed = [grid_speed(step, p) for p in range(2)] + [[zero] * 3]
         turned = [turn(speed[0]), turn(speed[1]), [zero] * 3]
-        for k in range(BLOCKS):
-            p = k // 4
-            windows(k, speed[p], turned[p], speed[p + 1], turned[p + 1])
-        for k in range(BLOCKS):
-            gather(k)
+        fields = []
         for j in range(TILES):
-            advance(j)
+            p = j // 2
+            for k in (2 * j, 2 * j + 1):
+                windows(k, speed[p], turned[p], speed[p + 1], turned[p + 1])
+                gather(k)
+            advance(j, last)
+            if not last:
+                fields.append(deposit_tile(j))
+        return fields
+
+    def one_step(step, carry):
+        send_all(step + 1, take(step, False))
+        start_all(step + 1)
         return carry
 
-    lax.fori_loop(0, STEPS, one_step, 0)
+    send_all(0, [deposit_tile(j) for j in range(TILES)])
+    pl.semaphore_wait(barrier, around)
+    start_all(0)
+    lax.fori_loop(0, STEPS - 1, one_step, 0)
+    take(STEPS - 1, True)
 
     each_edge(lambda rows: passed(send_sem, STEPS * rows))
-    live = live_ref[...]
-    for ref, count in ((off, 3), (vel, 3), (aff, 9), (frame, 9)):
-        for i in range(count):
-            ref[i] = ref[i] * live
 
 
 def write_out(off, vel, aff, frame, off_out, vel_out, aff_out, frame_out, sem):

time: 44 us -> 44.9 us (1.020)
  Pallas kernels: 43.2 us -> 44.1 us
    pallas_call x1, Pallas kernels: 42.5 us -> 43.4 us  [per_device(): pl.pallas_call(functools.partial(kernel, nx, ny), out_shape=[jax.ShapeDty...]
where the time goes in v8:
time: 44.9 us; the launch traced here: 44.8 us
  Pallas kernels  44.1 us (98%)
  between operations  0.64 us (1%)
    pallas_call x1, Pallas kernels, per_device(): pl.pallas_call(functools.partial(kernel, nx, ny), out_shape=[jax.ShapeDty...  43.4 us

profile of v8, /device:TPU:1, one launch (start us, length us, event | category | flops | bytes accessed | tf_op | source)
XLA Modules:
  0.0 44.8 jit_solution(9412894977649322895)
XLA Ops:
  0.6 43.4 %shard_map.102 = (f32[3,32,128]{2,1,0:T(8,128)S(1)}, f32[3,32,128]{2,1,0:T(8,128)S(1)}, f32[9,32,128]{2,1,0:T(8,128)S(1)}, f32[9,32,128]{2,1,0:T(8,128)S(1)}) custom-call(s32[8]{0:T(128)} %bitcast.17, f32[3,32,128]{2,1,0:T(8,128)} %bitcast.13, f32[3,32,128]{2,1,0:T(8,128)} %bitcast.14, f32[9,32,128]{2,1,0:T(8,128)} %bitcast.11, f32[9,32,128]{2,1,0:T(8,128)} %bitcast.12, ...), custom_call_target="tpu_custom_call" | custom-call | tf_op jit(solution)/shard_map/pallas_call | solution.py:405
  44.0 0.8 %shard_map.103 = (f32[3,32,128]{2,1,0:T(8,128)}, f32[3,32,128]{2,1,0:T(8,128)}, f32[9,32,128]{2,1,0:T(8,128)}, f32[9,32,128]{2,1,0:T(8,128)}) custom-call(f32[3,32,128]{2,1,0:T(8,128)S(1)} %get-tuple-element.12.off, f32[3,32,128]{2,1,0:T(8,128)S(1)} %get-tuple-element.13.vel, f32[9,32,128]{2,1,0:T(8,128)S(1)} %get-tuple-element.14.aff, ...), custom_call_target="tpu_custom_call" | custom-call | tf_op jit(solution)/shard_map/pallas_call | solution.py:456

commit v9 on v7

--- a/solution.py
+++ b/solution.py
@@ -96,11 +96,12 @@
             (vel_hbm, vel), (aff_hbm, aff), (strain_hbm, strain_in),
         ))
     ]
-    for load in loads:
-        load.start()
-
-    for ref in (recv_x, recv_low, recv_high, diag_low, diag_high):
-        ref[...] = jnp.zeros(ref.shape, ref.dtype)
+    def clear_step(step, carry):
+        for ref in (recv_x, recv_low, recv_high, diag_low, diag_high):
+            ref[step] = jnp.zeros(ref.shape[1:], ref.dtype)
+        return carry
+
+    lax.fori_loop(0, STEPS, clear_step, 0)
     barrier = pltpu.get_barrier_semaphore()
     around = jnp.int32(0)
     for dx, dy in DIRECTIONS:
@@ -111,8 +112,21 @@
         def _():
             pl.semaphore_signal(barrier, inc=1, device_id=neighbour(dx, dy), device_id_type=MESH)
 
-    for ref in (side_rows, plane_rows, us, bs):
-        ref[...] = jnp.zeros(ref.shape, ref.dtype)
+    for load in loads:
+        load.start()
+    blank = jnp.zeros((8, 128), jnp.float32)
+
+    def clear_tile(j, carry):
+        side_rows[j, 480:512, :] = jnp.zeros((32, 128), jnp.float32)
+        for odd in range(2):
+            for e in range(6):
+                for z in (6, 7):
+                    plane_rows[j, odd, pl.ds(8 * (8 * e + (z + 4 * odd) % 8), 8), :] = blank
+            for at in (48, 112):
+                bs[2 * j + odd, at : at + 16, :] = jnp.zeros((16, 512), jnp.bfloat16)
+        return carry
+
+    lax.fori_loop(0, TILES, clear_tile, 0)
     for load in loads:
         load.wait()
     row = iota((ROWS, 128), 0)
@@ -314,7 +328,7 @@
             s = CHUNKS * (k % 2) + c
             gathered[k // 2, pl.ds(s, 72, stride=8), :] = taken[:72, 128 * c : 128 * c + 128]
 
-    def advance(j):
+    def advance(j, step):
         rows = pl.ds(8 * j, 8)
         weights = [wx[j, e] for e in range(6)]
 
@@ -338,10 +352,10 @@
             for a in range(3)
             for b in range(3)
         ]
+        scale = jnp.where(step == STEPS - 1, live_ref[rows, :], 1.0)
         for ref, values in ((off, o), (vel, v), (aff, c), (frame, f)):
             for i, value in enumerate(values):
-                ref[i, rows, :] = value
-        return o, f, v, c
+                ref[i, rows, :] = value * scale
 
     def turn(values):
         return [pltpu.roll(value, 64, 1) for value in values]
@@ -366,16 +380,12 @@
         for k in range(BLOCKS):
             gather(k)
         for j in range(TILES):
-            advance(j)
+            advance(j, step)
         return carry
 
     lax.fori_loop(0, STEPS, one_step, 0)
 
     each_edge(lambda rows: passed(send_sem, STEPS * rows))
-    live = live_ref[...]
-    for ref, count in ((off, 3), (vel, 3), (aff, 9), (frame, 9)):
-        for i in range(count):
-            ref[i] = ref[i] * live
 
 
 def write_out(off, vel, aff, frame, off_out, vel_out, aff_out, frame_out, sem):

time: 44 us -> 44.2 us (level)
  no operation moved by 1% of the time
where the time goes in v9:
time: 44.2 us; the launch traced here: 44.1 us
  Pallas kernels  43.4 us (98%)
  between operations  0.64 us (1%)
    pallas_call x1, Pallas kernels, per_device(): pl.pallas_call(functools.partial(kernel, nx, ny), out_shape=[jax.ShapeDty...  42.7 us

profile of v9, /device:TPU:1, one launch (start us, length us, event | category | flops | bytes accessed | tf_op | source)
XLA Modules:
  0.0 44.1 jit_solution(10525100284514640565)
XLA Ops:
  0.6 42.7 %shard_map.102 = (f32[3,32,128]{2,1,0:T(8,128)S(1)}, f32[3,32,128]{2,1,0:T(8,128)S(1)}, f32[9,32,128]{2,1,0:T(8,128)S(1)}, f32[9,32,128]{2,1,0:T(8,128)S(1)}) custom-call(s32[8]{0:T(128)} %bitcast.17, f32[3,32,128]{2,1,0:T(8,128)} %bitcast.13, f32[3,32,128]{2,1,0:T(8,128)} %bitcast.14, f32[9,32,128]{2,1,0:T(8,128)} %bitcast.11, f32[9,32,128]{2,1,0:T(8,128)} %bitcast.12, ...), custom_call_target="tpu_custom_call" | custom-call | tf_op jit(solution)/shard_map/pallas_call | solution.py:409
  43.3 0.8 %shard_map.103 = (f32[3,32,128]{2,1,0:T(8,128)}, f32[3,32,128]{2,1,0:T(8,128)}, f32[9,32,128]{2,1,0:T(8,128)}, f32[9,32,128]{2,1,0:T(8,128)}) custom-call(f32[3,32,128]{2,1,0:T(8,128)S(1)} %get-tuple-element.12.off, f32[3,32,128]{2,1,0:T(8,128)S(1)} %get-tuple-element.13.vel, f32[9,32,128]{2,1,0:T(8,128)S(1)} %get-tuple-element.14.aff, ...), custom_call_target="tpu_custom_call" | custom-call | tf_op jit(solution)/shard_map/pallas_call | solution.py:460

commit v10 on v7

--- a/solution.py
+++ b/solution.py
@@ -247,36 +247,37 @@
         pair = [pairs[j, pl.ds(6 * i, 8), :] for i in range(10)]
         return [pair[0]] + [pair[1 + a] + ey * pair[4 + a] + ez * pair[7 + a] for a in range(3)]
 
+    def rolled(value, shift):
+        return value if shift % 128 == 0 else pltpu.roll(value, shift % 128, 1)
+
     def send(step, p, before, first, second):
         low, high = zero, zero
         for i in range(4):
             one = jnp.where(own, first[i], before[i])
             two = jnp.where(own, second[i], first[i])
-            mine = jnp.where(half, one, two) + pltpu.roll(jnp.where(half, two, one), 64, 1)
-            send_x[step, 4 * p + i] = mine
-            to_low = mine if i == 0 else pltpu.roll(mine, 16 * i, 1)
-            shift = (16 * i - 32) % 128
-            to_high = mine if shift == 0 else pltpu.roll(mine, shift, 1)
+            near, far = jnp.where(half, one, two), jnp.where(half, two, one)
+            send_x[step, 4 * p + i] = near + rolled(far, 64)
+            to_low = rolled(near, 16 * i) + rolled(far, 16 * i + 64)
+            to_high = rolled(near, 16 * i - 32) + rolled(far, 16 * i + 32)
             low = jnp.where(group == i, to_low, low)
             high = jnp.where(group == i, to_high, high)
         send_low[step, p] = low
         send_high[step, p] = high
 
-    def grid_speed(step, p):
+    def grid_speed(step, p, turn):
         below = recv_low[step, p] + diag_low[step, p]
         above = recv_high[step, p] + diag_high[step, p]
         total = []
         for i in range(4):
-            from_low = below if i == 0 else pltpu.roll(below, 128 - 16 * i, 1)
-            shift = (32 - 16 * i) % 128
-            from_high = above if shift == 0 else pltpu.roll(above, shift, 1)
+            from_low = rolled(below, turn - 16 * i)
+            from_high = rolled(above, turn + 32 - 16 * i)
             extra = jnp.where(group == 0, from_low, jnp.where(group == 2, from_high, 0.0))
-            total.append(send_x[step, 4 * p + i] + recv_x[step, 4 * p + i] + extra)
+            total.append(rolled(send_x[step, 4 * p + i] + recv_x[step, 4 * p + i], turn) + extra)
         scale = 1.0 / jnp.maximum(total[0], mass_floor)
         speed_x = total[1] * scale + time_step * gravity_slope
         speed_y = total[2] * scale
         speed_z = total[3] * scale + time_step * gravity_vertical
-        place_z = 16 * p + jnp.where(half, 0, 8) + r3
+        place_z = 16 * p + jnp.where(half, turn // 8, 8 - turn // 8) + r3
         speed_x = jnp.where(place_x < 2, jnp.maximum(speed_x, 0.0), speed_x)
         speed_x = jnp.where(place_x >= 4 * nx - 2, jnp.minimum(speed_x, 0.0), speed_x)
         speed_y = jnp.where(place_y < 2, jnp.maximum(speed_y, 0.0), speed_y)
@@ -343,9 +344,6 @@
                 ref[i, rows, :] = value
         return o, f, v, c
 
-    def turn(values):
-        return [pltpu.roll(value, 64, 1) for value in values]
-
     def one_step(step, carry):
         fields = [deposit_tile(j) for j in range(TILES)]
         send(step, 0, [zero] * 4, fields[0], fields[1])
@@ -358,8 +356,8 @@
         each_neighbour(lambda d: copy_to(step, d).start())
 
         each_edge(lambda rows: passed(recv_sem.at[step], rows))
-        speed = [grid_speed(step, p) for p in range(2)] + [[zero] * 3]
-        turned = [turn(speed[0]), turn(speed[1]), [zero] * 3]
+        speed = [grid_speed(step, p, 0) for p in range(2)] + [[zero] * 3]
+        turned = [grid_speed(step, p, 64) for p in range(2)] + [[zero] * 3]
         for k in range(BLOCKS):
             p = k // 4
             windows(k, speed[p], turned[p], speed[p + 1], turned[p + 1])

time: 44 us -> 43.4 us (0.986)
  Pallas kernels: 43.2 us -> 42.7 us
    pallas_call x1, Pallas kernels: 42.5 us -> 41.9 us  [per_device(): pl.pallas_call(functools.partial(kernel, nx, ny), out_shape=[jax.ShapeDty...]
where the time goes in v10:
time: 43.4 us; the launch traced here: 43.3 us
  Pallas kernels  42.7 us (98%)
  between operations  0.64 us (1%)
    pallas_call x1, Pallas kernels, per_device(): pl.pallas_call(functools.partial(kernel, nx, ny), out_shape=[jax.ShapeDty...  41.9 us

profile of v10, /device:TPU:1, one launch (start us, length us, event | category | flops | bytes accessed | tf_op | source)
XLA Modules:
  0.0 43.3 jit_solution(4012780118451979151)
XLA Ops:
  0.6 41.9 %shard_map.102 = (f32[3,32,128]{2,1,0:T(8,128)S(1)}, f32[3,32,128]{2,1,0:T(8,128)S(1)}, f32[9,32,128]{2,1,0:T(8,128)S(1)}, f32[9,32,128]{2,1,0:T(8,128)S(1)}) custom-call(s32[8]{0:T(128)} %bitcast.17, f32[3,32,128]{2,1,0:T(8,128)} %bitcast.13, f32[3,32,128]{2,1,0:T(8,128)} %bitcast.14, f32[9,32,128]{2,1,0:T(8,128)} %bitcast.11, f32[9,32,128]{2,1,0:T(8,128)} %bitcast.12, ...), custom_call_target="tpu_custom_call" | custom-call | tf_op jit(solution)/shard_map/pallas_call | solution.py:397
  42.5 0.8 %shard_map.103 = (f32[3,32,128]{2,1,0:T(8,128)}, f32[3,32,128]{2,1,0:T(8,128)}, f32[9,32,128]{2,1,0:T(8,128)}, f32[9,32,128]{2,1,0:T(8,128)}) custom-call(f32[3,32,128]{2,1,0:T(8,128)S(1)} %get-tuple-element.12.off, f32[3,32,128]{2,1,0:T(8,128)S(1)} %get-tuple-element.13.vel, f32[9,32,128]{2,1,0:T(8,128)S(1)} %get-tuple-element.14.aff, ...), custom_call_target="tpu_custom_call" | custom-call | tf_op jit(solution)/shard_map/pallas_call | solution.py:448
